TPU v7x, 32 devices: a whole 2x2x4 slice. The times are simulated.
32 devices in a mesh: dp: 8 (over z, x), tensor: 4 (over y, core).
Axes of the slice: x: 2, y: 2, z: 4, core: 2. Of those that a mesh axis runs over, the one named last changes fastest.
Arguments:
- inputs: bfloat16 [12288, 1024], P(('dp', 'tensor')), may hold values from -6 to 6
- output_grad: bfloat16 [12288, 1024], P(('dp', 'tensor')), may hold values from -12 to 12
- input_project: bfloat16 [3, 1024, 1024], P(None, None, 'tensor'), may hold values from -0.1875 to 0.1875
- output_project: bfloat16 [1024, 1024], P('tensor'), may hold values from -2 to 2
- expand_weight: bfloat16 [1024, 4096], P(None, 'tensor'), may hold values from -0.1875 to 0.1875
- reduce_weight: bfloat16 [4096, 1024], P('tensor'), may hold values from -0.09375 to 0.09375
- first_gain: float32 [1024], replicated, may hold values from 0.5 to 1.5
- second_gain: float32 [1024], replicated, may hold values from 0.5 to 1.5
- biases: float32 [160, 64], replicated, may hold values from -1.2 to 1.2
- first_moment: float32 [160, 64], replicated, may hold values from -1 to 1
- second_moment: float32 [160, 64], replicated, may hold values from 0.004003906 to 0.016113281
- left_pairs: float32 [32, 32], replicated, may hold values from -1 to 1, as said below
- left_hidden: float32 [64, 64], replicated, may hold values from -1 to 1, as said below
- left_small: float32 [4, 16, 16], replicated, may hold values from -1 to 1, as said below
- right_bases: float32 [6, 64, 64], replicated, may hold values from -1 to 1, as said below
- segment_number: int32 [12288], P('dp'), may hold values from 0 to 511, as said below
- token_mask: int32 [12288], P('dp'), may hold values from 0 to 1, as said below
- owners: int32 [6], replicated, may hold values from 0 to 7, as said below
Outputs:
- layer_out: bfloat16 [12288, 1024], P(('dp', 'tensor'))
- input_grad: bfloat16 [12288, 1024], P(('dp', 'tensor'))
- bias_grads: float32 [160, 64], replicated
- clip_norm: float32 [1], replicated
- new_biases: float32 [1280, 64], P('dp')
- bias_copies: bfloat16 [160, 64], replicated
- new_first: float32 [1280, 64], P('dp')
- new_second: float32 [1280, 64], P('dp')
Inputs may be any that keep to these rules, and one draw needn't show every extreme that they name: `segment_number`: within each packed row of 512 tokens the numbers start at 0 and never fall; the padding tail of a row, where token_mask is 0, has a number of its own. In one packed row every real token is a document of its own. `token_mask`: in each packed row the zeros form the tail. `owners`: six different dp indices, one for each bias matrix in the order of the views; 0, 4 and 7 are always among them. `left_pairs`: Orthogonal. `left_hidden`: Orthogonal. `left_small`: each matrix is orthogonal. `right_bases`: each matrix is orthogonal.
All inputs are finite; a program needn't handle non-finite values.
Results may differ from a plain program's by a relative error of at most 0.018.
Values may be sent and summed in bfloat16 or wider, within the bound.
A program may use at most 128 MiB of HBM per device.

v0:
```python
from functools import partial

import jax
import jax.numpy as jnp
from jax import lax
from jax.sharding import PartitionSpec as P

D = 1024
HEADS = 16
HD = 64
SEQ = 512
STEP = 10
FR = 64
DR = 16
BROWS = 160


EPS_NORM = 1e-12
CLIP_LIMIT = 64.0
BETA_ONE = 0.9
BETA_TWO = 0.99
ADAM_EPS = 1e-08
LEARN_RATE = 0.2
HIGHEST_PRECISION = lax.Precision.HIGHEST


def layer_norm(values, gain):
    centred = values - jnp.mean(values, axis=-1, keepdims=True)
    spread = jnp.mean(centred * centred, axis=-1, keepdims=True)
    return centred * lax.rsqrt(spread + EPS_NORM) * gain


def normed_back(values, gain, upstream):

    def inner(array):
        return layer_norm(array, gain)

    result, pullback = jax.vjp(inner, values)
    return pullback(upstream)[0]


def gelu_exact(values):
    return jax.nn.gelu(values, approximate=False)


def gelu_back(values, upstream):
    result, pullback = jax.vjp(gelu_exact, values)
    return pullback(upstream)[0]


def masked_scores(query, keys, allowed, score_scale):
    scores = (
        jnp.einsum("sqhd,skhd->shqk", query, keys, preferred_element_type=jnp.float32) * score_scale
    )
    return jnp.where(allowed[:, None], scores, -1e30)


def soap_update(grad_block, moment_one, moment_two, old_block, left_basis, right_basis):
    rotated = jnp.dot(
        jnp.dot(left_basis.T, grad_block, precision=HIGHEST_PRECISION),
        right_basis,
        precision=HIGHEST_PRECISION,
    )
    new_one = BETA_ONE * moment_one + (1.0 - BETA_ONE) * rotated
    new_two = BETA_TWO * moment_two + (1.0 - BETA_TWO) * rotated * rotated
    direction = (
        new_one / (1.0 - BETA_ONE**STEP) / (jnp.sqrt(new_two / (1.0 - BETA_TWO**STEP)) + ADAM_EPS)
    )
    turned = jnp.dot(
        jnp.dot(left_basis, direction, precision=HIGHEST_PRECISION),
        right_basis.T,
        precision=HIGHEST_PRECISION,
    )
    return (old_block - LEARN_RATE * turned, new_one, new_two)


def empty_triple(amount):
    nought = jnp.zeros((amount, HD), jnp.float32)
    return (nought, nought, nought)


def on_device(
    inputs,
    output_grad,
    input_project,
    output_project,
    expand_weight,
    reduce_weight,
    first_gain,
    second_gain,
    biases,
    first_moment,
    second_moment,
    left_pairs,
    left_hidden,
    left_small,
    right_bases,
    segment_number,
    token_mask,
    owners,
):
    tensor_rank = lax.axis_index("tensor")
    local_width = output_project.shape[0]
    local_heads = local_width // HD
    local_hidden = expand_weight.shape[1]
    token_rows = segment_number.shape[0]
    sequences = token_rows // SEQ
    score_scale = HD ** (-0.5)
    tail_start = 2 * HEADS + FR
    hidden_rows = local_hidden // HD
    query_bias = lax.dynamic_slice_in_dim(
        biases, tensor_rank * local_heads, local_heads, 0
    ).reshape(local_width)
    value_bias = lax.dynamic_slice_in_dim(
        biases, HEADS + tensor_rank * local_heads, local_heads, 0
    ).reshape(local_width)
    out_bias = biases[tail_start : tail_start + DR].reshape(D)
    first_shift = biases[tail_start + DR : tail_start + 2 * DR].reshape(D)
    ffn_bias = biases[tail_start + 2 * DR : tail_start + 3 * DR].reshape(D)
    second_shift = biases[tail_start + 3 * DR : tail_start + 4 * DR].reshape(D)
    full_inputs = lax.all_gather(inputs, "tensor", axis=0, tiled=True)
    projected = jnp.einsum(
        "td,cde->cte", full_inputs, input_project, preferred_element_type=jnp.float32
    )
    query_low = (
        (projected[0] + query_bias).astype(jnp.bfloat16).reshape(sequences, SEQ, local_heads, HD)
    )
    keys_low = projected[1].astype(jnp.bfloat16).reshape(sequences, SEQ, local_heads, HD)
    values_low = (
        (projected[2] + value_bias).astype(jnp.bfloat16).reshape(sequences, SEQ, local_heads, HD)
    )
    segments = segment_number.reshape(sequences, SEQ)
    valid = token_mask.reshape(sequences, SEQ)
    places = jnp.arange(SEQ, dtype=jnp.int32)
    allowed = (segments[:, :, None] == segments[:, None, :]) & (
        (valid[:, None, :] == 1) | (places[:, None] == places[None, :])[None]
    )
    scores = masked_scores(query_low, keys_low, allowed, score_scale)
    row_peak = jnp.max(scores, axis=-1, keepdims=True)
    row_total = jnp.sum(jnp.exp(scores - row_peak), axis=-1, keepdims=True)
    log_total = row_peak + jnp.log(row_total)
    probs_low = jnp.exp(scores - log_total).astype(jnp.bfloat16)
    context = jnp.einsum(
        "shqk,skhd->sqhd", probs_low, values_low, preferred_element_type=jnp.float32
    )
    context_low = context.reshape(token_rows, local_width).astype(jnp.bfloat16)
    portion = context_low
    attention_share = lax.psum_scatter(
        jnp.dot(portion, output_project, preferred_element_type=jnp.float32),
        "tensor",
        scatter_dimension=0,
        tiled=True,
    )
    first_pre = inputs.astype(jnp.float32) + attention_share + out_bias
    first_normed = layer_norm(first_pre, first_gain) + first_shift
    normed_low = first_normed.astype(jnp.bfloat16)
    hidden_bias = lax.dynamic_slice_in_dim(
        biases, 2 * HEADS + tensor_rank * hidden_rows, hidden_rows, 0
    ).reshape(local_hidden)
    hidden_pre = (
        jnp.dot(
            lax.all_gather(normed_low, "tensor", axis=0, tiled=True),
            expand_weight,
            preferred_element_type=jnp.float32,
        )
        + hidden_bias
    )
    hidden_low = gelu_exact(hidden_pre).astype(jnp.bfloat16)
    portion = hidden_low
    ffn_share = lax.psum_scatter(
        jnp.dot(portion, reduce_weight, preferred_element_type=jnp.float32).astype(jnp.bfloat16),
        "tensor",
        scatter_dimension=0,
        tiled=True,
    ).astype(jnp.float32)
    second_pre = first_normed + ffn_share + ffn_bias
    layer_out = (layer_norm(second_pre, second_gain) + second_shift).astype(jnp.bfloat16)
    upstream = output_grad.astype(jnp.float32)
    second_grad = normed_back(second_pre, second_gain, upstream)
    down_low = second_grad.astype(jnp.bfloat16)
    hidden_grad = jnp.einsum(
        "td,fd->tf",
        lax.all_gather(down_low, "tensor", axis=0, tiled=True),
        reduce_weight,
        preferred_element_type=jnp.float32,
    )
    pre_grad = gelu_back(hidden_pre, hidden_grad)
    pre_low = pre_grad.astype(jnp.bfloat16)
    portion = pre_low
    normed_part = lax.psum_scatter(
        jnp.einsum("tf,df->td", portion, expand_weight, preferred_element_type=jnp.float32).astype(
            jnp.bfloat16
        ),
        "tensor",
        scatter_dimension=0,
        tiled=True,
    ).astype(jnp.float32)
    hidden_start = 2 * HEADS + tensor_rank * hidden_rows
    normed_grad = second_grad + normed_part
    first_grad = normed_back(first_pre, first_gain, normed_grad)
    attention_grad_low = first_grad.astype(jnp.bfloat16)
    context_grad = jnp.einsum(
        "td,ed->te",
        lax.all_gather(attention_grad_low, "tensor", axis=0, tiled=True),
        output_project,
        preferred_element_type=jnp.float32,
    )
    context_grad_low = context_grad.astype(jnp.bfloat16).reshape(sequences, SEQ, local_heads, HD)
    scores = masked_scores(query_low, keys_low, allowed, score_scale)
    probs = jnp.exp(scores - log_total)
    prob_grad = jnp.einsum(
        "sqhd,skhd->shqk", context_grad_low, values_low, preferred_element_type=jnp.float32
    )
    row_delta = jnp.sum(probs * prob_grad, axis=-1, keepdims=True)
    score_grad = (probs * (prob_grad - row_delta)).astype(jnp.bfloat16)
    query_grad = (
        jnp.einsum("shqk,skhd->sqhd", score_grad, keys_low, preferred_element_type=jnp.float32)
        * score_scale
    )
    key_grad = (
        jnp.einsum("shqk,sqhd->skhd", score_grad, query_low, preferred_element_type=jnp.float32)
        * score_scale
    )
    value_grad = jnp.einsum(
        "shqk,sqhd->skhd", probs_low, context_grad_low, preferred_element_type=jnp.float32
    )
    stacked_low = (
        jnp.stack([query_grad, key_grad, value_grad])
        .reshape(3, token_rows, local_width)
        .astype(jnp.bfloat16)
    )
    portion = stacked_low
    input_share = lax.psum_scatter(
        jnp.einsum(
            "cte,cde->td", portion, input_project, preferred_element_type=jnp.float32
        ).astype(jnp.bfloat16),
        "tensor",
        scatter_dimension=0,
        tiled=True,
    ).astype(jnp.float32)
    input_grad = (first_grad + input_share).astype(jnp.bfloat16)
    zero_index = jnp.int32(0)
    bias_term = jnp.zeros((BROWS, HD), jnp.float32)
    bias_term = lax.dynamic_update_slice(
        bias_term, jnp.sum(query_grad, axis=(0, 1)), (tensor_rank * local_heads, zero_index)
    )
    bias_term = lax.dynamic_update_slice(
        bias_term, jnp.sum(value_grad, axis=(0, 1)), (HEADS + tensor_rank * local_heads, zero_index)
    )
    bias_term = lax.dynamic_update_slice(
        bias_term, jnp.sum(pre_grad, axis=0).reshape(-1, HD), (hidden_start, zero_index)
    )
    tail_sums = jnp.concatenate(
        [
            jnp.sum(first_grad, axis=0),
            jnp.sum(normed_grad, axis=0),
            jnp.sum(second_grad, axis=0),
            jnp.sum(upstream, axis=0),
        ]
    ).reshape(4 * DR, HD)
    bias_term = lax.dynamic_update_slice(bias_term, tail_sums, (jnp.int32(tail_start), zero_index))
    bias_share = lax.psum_scatter(
        bias_term.reshape(BROWS * HD), ("dp", "tensor"), scatter_dimension=0, tiled=True
    )
    squares = lax.psum(jnp.sum(bias_share * bias_share), ("dp", "tensor"))
    clip_norm = jnp.sqrt(squares)
    clipped_share = bias_share * (CLIP_LIMIT / jnp.maximum(clip_norm, CLIP_LIMIT))
    clipped = lax.all_gather(clipped_share, ("dp", "tensor"), axis=0, tiled=True).reshape(BROWS, HD)
    dp_rank = lax.axis_index("dp")
    layout = [(0, 2 * HEADS, left_pairs), (2 * HEADS, FR, left_hidden)]
    layout = layout + [(tail_start + which * DR, DR, left_small[which]) for which in range(4)]
    new_parts, one_parts, two_parts = ([], [], [])
    for which in range(6):
        begin, amount, left_basis = layout[which]
        owned = partial(
            soap_update,
            clipped[begin : begin + amount],
            first_moment[begin : begin + amount],
            second_moment[begin : begin + amount],
            biases[begin : begin + amount],
            left_basis,
            right_bases[which],
        )
        fresh, moment_one, moment_two = lax.cond(
            owners[which] == dp_rank, owned, partial(empty_triple, amount)
        )
        new_parts.append(fresh)
        one_parts.append(moment_one)
        two_parts.append(moment_two)
    new_owned = jnp.concatenate(new_parts, axis=0)
    first_owned = jnp.concatenate(one_parts, axis=0)
    second_owned = jnp.concatenate(two_parts, axis=0)
    fresh_all = lax.psum(new_owned.astype(jnp.bfloat16), "dp")
    return (
        layer_out,
        input_grad,
        clipped,
        clip_norm.reshape(1),
        new_owned,
        fresh_all,
        first_owned,
        second_owned,
    )


def solution(mesh):
    return jax.shard_map(
        on_device,
        mesh=mesh,
        in_specs=(
            P(("dp", "tensor"), None),
            P(("dp", "tensor"), None),
            P(None, None, "tensor"),
            P("tensor", None),
            P(None, "tensor"),
            P("tensor", None),
            P(),
            P(),
            P(),
            P(),
            P(),
            P(),
            P(),
            P(),
            P(),
            P("dp"),
            P("dp"),
            P(),
        ),
        out_specs=(
            P(("dp", "tensor"), None),
            P(("dp", "tensor"), None),
            P(),
            P(),
            P("dp", None),
            P(),
            P("dp", None),
            P("dp", None),
        ),
        check_vma=False,
    )
```

profile of v0, /device:TPU:0, one launch (start us, length us, event | category | flops | bytes accessed | tf_op | source)
XLA Modules:
  0.0 617.0 jit_solution(13239431366007767052)
XLA Ops:
  11.4 29.4 %all-gather.5.cloned.1.call-done = bf16[1536,1024]{1,0:T(8,128)(2,1)} async-done(((bf16[384,1024]{1,0:T(8,128)(2,1)}), bf16[1536,1024]{1,0:T(8,128)(2,1)}) %all-gather.5.cloned.1.call-update) | async-done | bytes 3145744 | tf_op jit(solution)/shard_map/all_gather | solution.py:121
  40.8 5.0 convolution_bitcast_fusion
  48.7 3.9 squeeze.63
  56.2 3.9 squeeze.64
  62.1 4.3 fusion.140
  71.4 3.9 fusion.160
  83.8 54.6 %reduce-scatter.5.cloned.1.call-done = f32[384,1024]{1,0:T(8,128)} async-done(((f32[1536,1024]{1,0:T(8,128)}), f32[384,1024]{1,0:T(8,128)}) %reduce-scatter.5.cloned.1.call-update) | async-done | bytes 1572880 | tf_op jit(solution)/shard_map/reduce_scatter | solution.py:148
  145.6 25.9 %all-gather.7.cloned.1.call-done = bf16[1536,1024]{1,0:T(8,128)(2,1)} async-done(((bf16[384,1024]{1,0:T(8,128)(2,1)}), bf16[1536,1024]{1,0:T(8,128)(2,1)}) %all-gather.7.cloned.1.call-update) | async-done | bytes 3145744 | tf_op jit(solution)/shard_map/all_gather | solution.py:162
  171.5 17.4 %fusion.142 = (f32[1536,1024]{1,0:T(8,128)S(1)}, f32[1536,1024]{1,0:T(8,128)S(1)}) fusion(f32[1024]{0:T(1024)} %add.220, bf16[1536,1024]{1,0:T(8,128)(2,1)} %all-gather.7.cloned.1.call-done, bf16[1024,1024]{1,0:T(8,128)(2,1)S(1)} %copy-done), kind=kOutput, calls=%fused_computation.172 | convolution fusion | flops 3320315904 | bytes 17829888 | tf_op jit(solution)/shard_map/dot_general | solution.py:161
  193.4 4.8 convolution_convert_fusion.1
  199.9 36.4 %reduce-scatter.7.cloned.1.call-done = bf16[384,1024]{1,0:T(8,128)(2,1)} async-done(((bf16[1536,1024]{1,0:T(8,128)(2,1)}), bf16[384,1024]{1,0:T(8,128)(2,1)}) %reduce-scatter.7.cloned.1.call-update) | async-done | bytes 786448 | tf_op jit(solution)/shard_map/reduce_scatter | solution.py:170
  244.5 28.5 %all-gather.9.cloned.1.call-done = bf16[1536,1024]{1,0:T(8,128)(2,1)} async-done(((bf16[384,1024]{1,0:T(8,128)(2,1)}), bf16[1536,1024]{1,0:T(8,128)(2,1)}) %all-gather.9.cloned.1.call-update) | async-done | bytes 3145744 | tf_op jit(solution)/shard_map/all_gather | solution.py:183
  273.0 12.4 %fusion.179 = (f32[1024]{0:T(1024)}, bf16[1536,1024]{1,0:T(8,128)(2,1)S(1)}) fusion(f32[1536,1024]{1,0:T(8,128)} %copy-done.40, f32[1536,1024]{1,0:T(8,128)} %copy-done.41, f32[1024]{0:T(1024)} %add.220, bf16[1536,1024]{1,0:T(8,128)(2,1)} %all-gather.9.cloned.1.call-done, bf16[1024,1024]{1,0:T(8,128)(2,1)} %param.35), kind=kOutput, calls=%fused_computation.270 | convolution fusion | flops 3246390272 | bytes 20979712 | tf_op jit(solution)/shard_map/td,fd->tf/dot_general | solution.py:181
  285.4 5.0 convolution_convert_fusion
  290.5 38.0 %reduce-scatter.9.cloned.1.call-done = bf16[384,1024]{1,0:T(8,128)(2,1)} async-done(((bf16[1536,1024]{1,0:T(8,128)(2,1)}), bf16[384,1024]{1,0:T(8,128)(2,1)}) %reduce-scatter.9.cloned.1.call-update) | async-done | bytes 786448 | tf_op jit(solution)/shard_map/reduce_scatter | solution.py:190
  335.8 28.6 %all-gather.11.cloned.1.call-done = bf16[1536,1024]{1,0:T(8,128)(2,1)} async-done(((bf16[384,1024]{1,0:T(8,128)(2,1)}), bf16[1536,1024]{1,0:T(8,128)(2,1)}) %all-gather.11.cloned.1.call-update) | async-done | bytes 3145744 | tf_op jit(solution)/shard_map/all_gather | solution.py:204
  375.4 9.7 %bitcast_convert_fusion.1 = (bf16[3,512,4,64]{1,3,2,0:T(8,128)(2,1)}, f32[3,4,64,512]{3,2,1,0:T(8,128)}) fusion(bf16[3,512,4,64]{1,3,2,0:T(8,128)(2,1)} %copy.152, f32[3,4,512,512]{2,3,1,0:T(8,128)} %copy-done.1, f32[3,4,512]{2,1,0:T(4,128)S(1)} %log_add_fusion, pred[3,512,512]{1,2,0:T(8,128)(4,1)S(1)} %or_and_fusion), kind=kOutput, calls=%fused_computation.214 | convolution fusion | flops 415629312 | bytes 16539648 | tf_op jit(solution)/shard_map/shqk,sqhd->skhd/dot_general | solution.py:224
  385.1 9.9 %multiply_reduce_fusion = (f32[3,4,512]{2,1,0:T(4,128)S(1)}, f32[3,4,512,512]{2,3,1,0:T(8,128)}) fusion(f32[3,4,512,512]{2,3,1,0:T(8,128)} %copy-done.1, f32[3,4,512]{2,1,0:T(4,128)S(1)} %log_add_fusion, pred[3,512,512]{1,2,0:T(8,128)(4,1)S(1)} %or_and_fusion, bf16[3,512,4,64]{1,3,2,0:T(8,128)(2,1)S(1)} %copy-done.13, ...), kind=kOutput, calls=%fused_computation.165 | convolution fusion | flops 418375680 | bytes 27574272 | tf_op jit(solution)/shard_map/sqhd,skhd->shqk/dot_general | solution.py:211
  395.0 7.0 %multiply_convert_fusion = bf16[3,4,512,512]{2,3,1,0:T(8,128)(2,1)S(1)} fusion(f32[3,4,512,512]{2,3,1,0:T(8,128)} %get-tuple-element.399, f32[3,4,512,512]{2,3,1,0:T(8,128)S(1)} %bitcast.137, f32[3,4,512]{2,1,0:T(4,128)S(1)} %get-tuple-element.398, f32[3,4,512]{2,1,0:T(4,128)S(1)} %log_add_fusion, pred[3,512,512]{1,2,0:T(8,128)(4,1)S(1)} %or_and_fusion), kind=kLoop, calls=%fused_computation.164 | loop fusion | flops 18874368 | bytes 32292864 | tf_op jit(solution)/shard_map/convert_element_type | solution.py:215
  426.7 6.2 %bitcast_convert_fusion = bf16[1536,1024]{1,0:T(8,128)(2,1)} fusion(bf16[3,1024,256]{2,1,0:T(8,128)(2,1)} %param.32, bf16[1,1536,256]{2,1,0:T(8,128)(2,1)S(1)} %copy-done.19, bf16[1,1536,256]{2,1,0:T(8,128)(2,1)} %reshape.226, bf16[1,1536,256]{2,1,0:T(8,128)(2,1)} %reshape.225), kind=kOutput, calls=%fused_computation.173 | convolution fusion | flops 2419851264 | bytes 7077888 | tf_op jit(solution)/shard_map/cte,cde->td/dot_general | solution.py:234
  441.6 40.2 %all-reduce.1 = f32[10240]{0:T(1024)S(1)} all-reduce(f32[10240]{0:T(1024)S(1)} %reshape.218), channel_id=6, replica_groups=mesh['dp'=8,'tensor'=4] {'dp','tensor'}, use_global_device_ids=true, to_apply=%region_22.23.clone | all-reduce | flops 10240 | bytes 81920
  482.4 41.2 %psum.14 = f32[]{:T(128)} all-reduce(f32[]{:T(128)} %multiply_reduce_fusion.4), channel_id=1, replica_groups=mesh['dp'=8,'tensor'=4] {'dp','tensor'}, use_global_device_ids=true, to_apply=%region_24.25 | all-reduce | flops 1 | bytes 8 | tf_op jit(solution)/shard_map/psum | solution.py:265
  524.6 39.6 %all-reduce = f32[10240]{0:T(1024)S(1)} all-reduce(f32[10240]{0:T(1024)S(1)} %multiply_dynamic-update-slice_fusion), channel_id=1, replica_groups=mesh['dp'=8,'tensor'=4] {'dp','tensor'}, use_global_device_ids=true, to_apply=%add | all-reduce | flops 10240 | bytes 81920
  568.1 37.7 %psum.15 = bf16[160,64]{0,1:T(8,128)(2,1)} all-reduce(bf16[160,64]{0,1:T(8,128)(2,1)S(1)} %convert_element_type.128), channel_id=1, replica_groups=mesh['dp'=8,'tensor'=4] {'dp'}, use_global_device_ids=true, to_apply=%region_37.38 | all-reduce | flops 10240 | bytes 40960 | tf_op jit(solution)/shard_map/psum | solution.py:293
  (221 shorter events, 103.9 us)
Async XLA Ops:
  7.2 164.3 %copy-start = (bf16[1024,1024]{1,0:T(8,128)(2,1)S(1)}, bf16[1024,1024]{1,0:T(8,128)(2,1)}, u32[]{:S(2)}) copy-start(bf16[1024,1024]{1,0:T(8,128)(2,1)} %param.34) | copy-start | bytes 6291460
  7.2 33.7 %all-gather.5.cloned.1.call-start = ((), (), s32[]{:S(2)}) async-start(), calls=%async_computation.4 | async-start | bytes 3932160 | tf_op jit(solution)/shard_map/all_gather | solution.py:121
  7.9 130.5 %reduce-scatter.5.cloned.1.call-start = ((), (), s32[]{:S(2)}) async-start(), calls=%async_computation.5 | async-start | bytes 7864320 | tf_op jit(solution)/shard_map/reduce_scatter | solution.py:148
  79.8 61.7 %copy-start.26 = (f32[1024]{0:T(1024)S(1)}, f32[1024]{0:T(1024)}, u32[]{:S(2)}) copy-start(f32[1024]{0:T(1024)} %param.36) | copy-start | bytes 12292
  79.9 91.6 %all-gather.7.cloned.1.call-start = ((), (), s32[]{:S(2)}) async-start(), calls=%async_computation.6 | async-start | bytes 3932160 | tf_op jit(solution)/shard_map/all_gather | solution.py:162
  82.2 58.1 %copy-start.24 = (f32[16,64]{1,0:T(8,128)}, f32[16,64]{1,0:T(8,128)S(1)}, u32[]{:S(2)}) copy-start(f32[16,64]{1,0:T(8,128)S(1)} %copy.248) | copy-start | bytes 12292
  83.8 105.1 %copy-start.27 = (f32[1024]{0:T(1024)}, f32[1024]{0:T(1024)S(1)}, u32[]{:S(2)}) copy-start(f32[1024]{0:T(1024)S(1)} %add.215) | copy-start | bytes 12292
  141.5 47.4 %copy-start.28 = (f32[384]{0:T(512)}, f32[384]{0:T(512)S(1)}, u32[]{:S(2)}) copy-start(f32[384]{0:T(512)S(1)} %fusion.171) | copy-start | bytes 4612
  142.7 93.6 %reduce-scatter.7.cloned.1.call-start = ((), (), s32[]{:S(2)}) async-start(), calls=%async_computation.7 | async-start | bytes 3932160 | tf_op jit(solution)/shard_map/reduce_scatter | solution.py:170
  198.2 74.8 %all-gather.9.cloned.1.call-start = ((), (), s32[]{:S(2)}) async-start(), calls=%async_computation.8 | async-start | bytes 3932160 | tf_op jit(solution)/shard_map/all_gather | solution.py:183
  244.3 84.2 %reduce-scatter.9.cloned.1.call-start = ((), (), s32[]{:S(2)}) async-start(), calls=%async_computation.9 | async-start | bytes 3932160 | tf_op jit(solution)/shard_map/reduce_scatter | solution.py:190
  290.4 41.1 %copy-start.33 = (f32[384]{0:T(512)S(1)}, f32[384]{0:T(512)}, u32[]{:S(2)}) copy-start(f32[384]{0:T(512)} %copy-done.32) | copy-start | bytes 4612
  290.4 41.1 %copy-start.29 = (f32[384]{0:T(512)S(1)}, f32[384]{0:T(512)}, u32[]{:S(2)}) copy-start(f32[384]{0:T(512)} %copy-done.28) | copy-start | bytes 4612
  290.4 74.1 %all-gather.11.cloned.1.call-start = ((), (), s32[]{:S(2)}) async-start(), calls=%async_computation.10 | async-start | bytes 3932160 | tf_op jit(solution)/shard_map/all_gather | solution.py:204
  335.8 270.0 %reduce-scatter.11.cloned.1.call-start = ((), (), s32[]{:S(2)}) async-start(), calls=%async_computation.11 | async-start | bytes 3932160 | tf_op jit(solution)/shard_map/reduce_scatter | solution.py:233
  432.9 132.0 %copy-start.15 = (f32[160,64]{0,1:T(8,128)S(1)}, f32[160,64]{0,1:T(8,128)}, u32[]{:S(2)}) copy-start(f32[160,64]{0,1:T(8,128)} %param.39) | copy-start | bytes 122884
  432.9 132.0 %copy-start.16 = (f32[160,64]{0,1:T(8,128)S(1)}, f32[160,64]{0,1:T(8,128)}, u32[]{:S(2)}) copy-start(f32[160,64]{0,1:T(8,128)} %param.40) | copy-start | bytes 122884
  432.9 132.0 %copy-start.18 = (f32[6,64,64]{2,1,0:T(8,128)S(1)}, f32[6,64,64]{2,1,0:T(8,128)}, u32[]{:S(2)}) copy-start(f32[6,64,64]{2,1,0:T(8,128)} %param.44) | copy-start | bytes 294916
  432.9 132.0 %copy-start.36 = (f32[32,32]{1,0:T(8,128)S(1)}, f32[32,32]{1,0:T(8,128)}, u32[]{:S(2)}) copy-start(f32[32,32]{1,0:T(8,128)} %param.41) | copy-start | bytes 12292
  432.9 132.0 %copy-start.30 = (f32[64,64]{1,0:T(8,128)S(1)}, f32[64,64]{1,0:T(8,128)}, u32[]{:S(2)}) copy-start(f32[64,64]{1,0:T(8,128)} %param.42) | copy-start | bytes 49156
  432.9 132.1 %copy-start.25 = (f32[16,64]{1,0:T(8,128)S(1)}, f32[16,64]{1,0:T(8,128)}, u32[]{:S(2)}) copy-start(f32[16,64]{1,0:T(8,128)} %copy-done.24) | copy-start | bytes 12292
  432.9 132.1 %copy-start.31 = (f32[4,16,16]{2,1,0:T(8,128)S(1)}, f32[4,16,16]{2,1,0:T(8,128)}, u32[]{:S(2)}) copy-start(f32[4,16,16]{2,1,0:T(8,128)} %param.43) | copy-start | bytes 12292
  433.0 132.2 %copy-start.23 = (f32[16,64]{1,0:T(8,128)S(1)}, f32[16,64]{1,0:T(8,128)}, u32[]{:S(2)}) copy-start(f32[16,64]{1,0:T(8,128)} %copy-done.22) | copy-start | bytes 12292
  566.6 42.0 %copy-start.21 = (f32[160,64]{0,1:T(8,128)}, f32[160,64]{0,1:T(8,128)S(1)}, u32[]{:S(2)}) copy-start(f32[160,64]{0,1:T(8,128)S(1)} %concatenate.28) | copy-start | bytes 122884
  (29 other events, 234.7 us)
Sparse Core Ops, SparseCore 0:
  9.6 31.2 all-gather.4
  80.0 58.3 reduce-scatter.4
  142.9 28.5 all-gather.6
  198.3 37.9 reduce-scatter.6
  244.4 28.5 all-gather.8
  290.5 37.9 reduce-scatter.8
  335.9 28.5 all-gather.10
  433.1 38.1 reduce-scatter.10
where the time goes:
time: 627 us; the launch traced here: 617 us
  waiting for transfers between devices  242 us (39%)
  blocking collectives  159 us (25%)
  matrix products  91.1 us (15%)
  local copies, waits for them, and re-layouts  66.1 us (11%)
  other arithmetic  37.2 us (6%)
  between operations  21 us (3%)
    unnamed x2, blocking collectives  79.7 us
    reduce_scatter x1, waiting for transfers between devices, on_device(): lax.psum_scatter(jnp.dot(portion, output_project, preferred_element_type=...  54.6 us
    psum x1, blocking collectives, on_device(): squares = lax.psum(jnp.sum(bias_share * bias_share), ('dp', 'tensor'))  41.2 us
    reduce_scatter x1, waiting for transfers between devices, on_device(): lax.psum_scatter(jnp.einsum('tf,df->td', portion, expand_weight, preferre...  38 us
    psum x1, blocking collectives, on_device(): fresh_all = lax.psum(new_owned.astype(jnp.bfloat16), 'dp')  37.7 us
    reduce_scatter x1, waiting for transfers between devices, on_device(): lax.psum_scatter(jnp.dot(portion, reduce_weight, preferred_element_type=j...  36.4 us
    all_gather x1, waiting for transfers between devices, on_device(): full_inputs = lax.all_gather(inputs, 'tensor', axis=0, tiled=True)  29.4 us
    all_gather x1, waiting for transfers between devices, on_device(): lax.all_gather(attention_grad_low, 'tensor', axis=0, tiled=True)  28.6 us
  transfers between devices with their start and end apart: 8, of which 7 were waited for; matrix products, arithmetic and copies ran while one was open for 3% of the time, Pallas kernels for 0%

commit v1 on v0

--- a/solution.py
+++ b/solution.py
@@ -1,5 +1,3 @@
-from functools import partial
-
 import jax
 import jax.numpy as jnp
 from jax import lax
@@ -72,11 +70,6 @@
         precision=HIGHEST_PRECISION,
     )
     return (old_block - LEARN_RATE * turned, new_one, new_two)
-
-
-def empty_triple(amount):
-    nought = jnp.zeros((amount, HD), jnp.float32)
-    return (nought, nought, nought)
 
 
 def on_device(
@@ -259,21 +252,16 @@
         ]
     ).reshape(4 * DR, HD)
     bias_term = lax.dynamic_update_slice(bias_term, tail_sums, (jnp.int32(tail_start), zero_index))
-    bias_share = lax.psum_scatter(
-        bias_term.reshape(BROWS * HD), ("dp", "tensor"), scatter_dimension=0, tiled=True
-    )
-    squares = lax.psum(jnp.sum(bias_share * bias_share), ("dp", "tensor"))
-    clip_norm = jnp.sqrt(squares)
-    clipped_share = bias_share * (CLIP_LIMIT / jnp.maximum(clip_norm, CLIP_LIMIT))
-    clipped = lax.all_gather(clipped_share, ("dp", "tensor"), axis=0, tiled=True).reshape(BROWS, HD)
+    bias_total = lax.psum(bias_term, ("dp", "tensor"))
+    clip_norm = jnp.sqrt(jnp.sum(bias_total * bias_total))
+    clipped = bias_total * (CLIP_LIMIT / jnp.maximum(clip_norm, CLIP_LIMIT))
     dp_rank = lax.axis_index("dp")
     layout = [(0, 2 * HEADS, left_pairs), (2 * HEADS, FR, left_hidden)]
     layout = layout + [(tail_start + which * DR, DR, left_small[which]) for which in range(4)]
-    new_parts, one_parts, two_parts = ([], [], [])
+    new_parts, one_parts, two_parts, owned_rows = ([], [], [], [])
     for which in range(6):
         begin, amount, left_basis = layout[which]
-        owned = partial(
-            soap_update,
+        fresh, moment_one, moment_two = soap_update(
             clipped[begin : begin + amount],
             first_moment[begin : begin + amount],
             second_moment[begin : begin + amount],
@@ -281,16 +269,16 @@
             left_basis,
             right_bases[which],
         )
-        fresh, moment_one, moment_two = lax.cond(
-            owners[which] == dp_rank, owned, partial(empty_triple, amount)
-        )
         new_parts.append(fresh)
         one_parts.append(moment_one)
         two_parts.append(moment_two)
-    new_owned = jnp.concatenate(new_parts, axis=0)
-    first_owned = jnp.concatenate(one_parts, axis=0)
-    second_owned = jnp.concatenate(two_parts, axis=0)
-    fresh_all = lax.psum(new_owned.astype(jnp.bfloat16), "dp")
+        owned_rows.append(jnp.full((amount, 1), owners[which] == dp_rank))
+    new_all = jnp.concatenate(new_parts, axis=0)
+    mine = jnp.concatenate(owned_rows, axis=0)
+    new_owned = jnp.where(mine, new_all, 0.0)
+    first_owned = jnp.where(mine, jnp.concatenate(one_parts, axis=0), 0.0)
+    second_owned = jnp.where(mine, jnp.concatenate(two_parts, axis=0), 0.0)
+    fresh_all = new_all.astype(jnp.bfloat16)
     return (
         layer_out,
         input_grad,

time: 627 us -> 507 us (0.81)
  blocking collectives: 159 us -> 39.8 us
    unnamed x2 -> x0, blocking collectives: 79.7 us -> none
    psum x2 -> x1, blocking collectives: 78.8 us -> 39.8 us  [on_device(): bias_total = lax.psum(bias_term, ('dp', 'tensor'))]
    all_gather x1, waiting for transfers between devices: 28.6 us -> 22.1 us  [on_device(): lax.all_gather(attention_grad_low, 'tensor', axis=0, tiled=True)]
    unnamed x97 -> x84, local copies, waits for them, and re-layouts: 13.8 us -> 11.5 us
  transfers between devices with their start and end apart: 8 -> 8, of which waited for: 7 -> 7; matrix products, arithmetic and copies ran while one was open for 3% -> 4% of each run, Pallas kernels for 0% -> 0%
where the time goes in v1:
time: 507 us; the launch traced here: 497 us
  waiting for transfers between devices  243 us (48%)
  matrix products  94.3 us (19%)
  local copies, waits for them, and re-layouts  61.8 us (12%)
  blocking collectives  39.8 us (8%)
  other arithmetic  37.4 us (7%)
  between operations  21 us (4%)
    reduce_scatter x1, waiting for transfers between devices, on_device(): lax.psum_scatter(jnp.dot(portion, output_project, preferred_element_type=...  57.3 us
    psum x1, blocking collectives, on_device(): bias_total = lax.psum(bias_term, ('dp', 'tensor'))  39.8 us
    reduce_scatter x1, waiting for transfers between devices, on_device(): lax.psum_scatter(jnp.einsum('tf,df->td', portion, expand_weight, preferre...  38.1 us
    reduce_scatter x1, waiting for transfers between devices, on_device(): lax.psum_scatter(jnp.dot(portion, reduce_weight, preferred_element_type=j...  37.8 us
    all_gather x1, waiting for transfers between devices, on_device(): full_inputs = lax.all_gather(inputs, 'tensor', axis=0, tiled=True)  29.4 us
    all_gather x1, waiting for transfers between devices, on_device(): lax.all_gather(normed_low, 'tensor', axis=0, tiled=True)  28.5 us
    all_gather x1, waiting for transfers between devices, on_device(): lax.all_gather(down_low, 'tensor', axis=0, tiled=True)  28.5 us
    all_gather x1, waiting for transfers between devices, on_device(): lax.all_gather(attention_grad_low, 'tensor', axis=0, tiled=True)  22.1 us
  transfers between devices with their start and end apart: 8, of which 7 were waited for; matrix products, arithmetic and copies ran while one was open for 4% of the time, Pallas kernels for 0%

profile of v1, /device:TPU:0, one launch (start us, length us, event | category | flops | bytes accessed | tf_op | source)
XLA Modules:
  0.0 497.4 jit_solution(15971714605525534313)
XLA Ops:
  11.4 29.4 %all-gather.5.cloned.1.call-done = bf16[1536,1024]{1,0:T(8,128)(2,1)} async-done(((bf16[384,1024]{1,0:T(8,128)(2,1)}), bf16[1536,1024]{1,0:T(8,128)(2,1)}) %all-gather.5.cloned.1.call-update) | async-done | bytes 3145744 | tf_op jit(solution)/shard_map/all_gather | solution.py:114
  40.8 5.0 %convolution_bitcast_fusion = f32[3,1536,256]{1,2,0:T(8,128)S(1)} fusion(bf16[3,1024,256]{2,1,0:T(8,128)(2,1)} %param.20, bf16[1536,1024]{1,0:T(8,128)(2,1)} %all-gather.5.cloned.1.call-done), kind=kOutput, calls=%fused_computation.27 | convolution fusion | flops 2415919104 | bytes 9437184 | tf_op jit(solution)/shard_map/td,cde->cte/dot_general | solution.py:115
  48.7 3.9 squeeze.55
  56.1 3.9 squeeze.56
  62.1 4.3 fusion
  71.4 3.9 fusion.20
  81.1 57.3 %reduce-scatter.5.cloned.1.call-done = f32[384,1024]{1,0:T(8,128)} async-done(((f32[1536,1024]{1,0:T(8,128)}), f32[384,1024]{1,0:T(8,128)}) %reduce-scatter.5.cloned.1.call-update) | async-done | bytes 1572880 | tf_op jit(solution)/shard_map/reduce_scatter | solution.py:141
  143.0 28.5 %all-gather.7.cloned.1.call-done = bf16[1536,1024]{1,0:T(8,128)(2,1)} async-done(((bf16[384,1024]{1,0:T(8,128)(2,1)}), bf16[1536,1024]{1,0:T(8,128)(2,1)}) %all-gather.7.cloned.1.call-update) | async-done | bytes 3145744 | tf_op jit(solution)/shard_map/all_gather | solution.py:155
  171.5 17.4 %fusion.2 = (f32[1536,1024]{1,0:T(8,128)S(1)}, f32[1536,1024]{1,0:T(8,128)S(1)}) fusion(f32[1024]{0:T(1024)S(1)} %add.222, bf16[1536,1024]{1,0:T(8,128)(2,1)} %all-gather.7.cloned.1.call-done, bf16[1024,1024]{1,0:T(8,128)(2,1)S(1)} %copy-done), kind=kOutput, calls=%fused_computation.8 | convolution fusion | flops 3320315904 | bytes 17829888 | tf_op jit(solution)/shard_map/dot_general | solution.py:154
  193.4 4.8 convolution_convert_fusion.1
  198.5 37.8 %reduce-scatter.7.cloned.1.call-done = bf16[384,1024]{1,0:T(8,128)(2,1)} async-done(((bf16[1536,1024]{1,0:T(8,128)(2,1)}), bf16[384,1024]{1,0:T(8,128)(2,1)}) %reduce-scatter.7.cloned.1.call-update) | async-done | bytes 786448 | tf_op jit(solution)/shard_map/reduce_scatter | solution.py:163
  244.5 28.5 %all-gather.9.cloned.1.call-done = bf16[1536,1024]{1,0:T(8,128)(2,1)} async-done(((bf16[384,1024]{1,0:T(8,128)(2,1)}), bf16[1536,1024]{1,0:T(8,128)(2,1)}) %all-gather.9.cloned.1.call-update) | async-done | bytes 3145744 | tf_op jit(solution)/shard_map/all_gather | solution.py:176
  272.9 11.8 %fusion.181 = (f32[1024]{0:T(1024)S(1)}, bf16[1536,1024]{1,0:T(8,128)(2,1)S(1)}) fusion(f32[1536,1024]{1,0:T(8,128)} %copy-done.29, f32[1536,1024]{1,0:T(8,128)} %copy-done.30, f32[1024]{0:T(1024)S(1)} %add.222, bf16[1536,1024]{1,0:T(8,128)(2,1)} %all-gather.9.cloned.1.call-done, bf16[1024,1024]{1,0:T(8,128)(2,1)} %param.23), kind=kOutput, calls=%fused_computation.266 | convolution fusion | flops 3246390272 | bytes 20979712 | tf_op jit(solution)/shard_map/td,fd->tf/dot_general | solution.py:174
  284.8 5.0 %convolution_convert_fusion = bf16[1536,1024]{1,0:T(8,128)(2,1)} fusion(bf16[1024,1024]{1,0:T(8,128)(2,1)S(1)} %copy-done, bf16[1536,1024]{1,0:T(8,128)(2,1)S(1)} %get-tuple-element.15), kind=kOutput, calls=%fused_computation.25 | convolution fusion | flops 3222798336 | bytes 8388608 | tf_op jit(solution)/shard_map/tf,df->td/dot_general | solution.py:184
  289.8 38.1 %reduce-scatter.9.cloned.1.call-done = bf16[384,1024]{1,0:T(8,128)(2,1)} async-done(((bf16[1536,1024]{1,0:T(8,128)(2,1)}), bf16[384,1024]{1,0:T(8,128)(2,1)}) %reduce-scatter.9.cloned.1.call-update) | async-done | bytes 786448 | tf_op jit(solution)/shard_map/reduce_scatter | solution.py:183
  341.9 22.1 %all-gather.11.cloned.1.call-done = bf16[1536,1024]{1,0:T(8,128)(2,1)} async-done(((bf16[384,1024]{1,0:T(8,128)(2,1)}), bf16[1536,1024]{1,0:T(8,128)(2,1)}) %all-gather.11.cloned.1.call-update) | async-done | bytes 3145744 | tf_op jit(solution)/shard_map/all_gather | solution.py:197
  363.9 3.9 convolution_convert_fusion.2
  367.8 3.7 reshape.160
  374.9 9.7 %bitcast_convert_fusion.1 = (bf16[3,512,4,64]{1,3,2,0:T(8,128)(2,1)}, f32[3,4,64,512]{3,2,1,0:T(8,128)}) fusion(bf16[3,512,4,64]{1,3,2,0:T(8,128)(2,1)} %copy.187, f32[3,4,512,512]{2,3,1,0:T(8,128)} %copy-done.1, f32[3,4,512]{2,1,0:T(4,128)S(1)} %log_add_fusion, pred[3,512,512]{1,2,0:T(8,128)(4,1)S(1)} %or_and_fusion), kind=kOutput, calls=%fused_computation.50 | convolution fusion | flops 415629312 | bytes 16539648 | tf_op jit(solution)/shard_map/shqk,sqhd->skhd/dot_general | solution.py:217
  384.6 9.8 %multiply_reduce_fusion = (f32[3,4,512]{2,1,0:T(4,128)S(1)}, f32[3,4,512,512]{2,3,1,0:T(8,128)}) fusion(f32[3,4,512,512]{2,3,1,0:T(8,128)} %copy-done.1, f32[3,4,512]{2,1,0:T(4,128)S(1)} %log_add_fusion, pred[3,512,512]{1,2,0:T(8,128)(4,1)S(1)} %or_and_fusion, bf16[3,512,4,64]{1,3,2,0:T(8,128)(2,1)S(1)} %copy-done.13, bf16[3,512,4,64]{1,0,3,2:T(4,128)(2,1)S(1)} %copy-done.11), kind=kOutput, calls=%fused_computation.1 | convolution fusion | flops 418375680 | bytes 27574272 | tf_op jit(solution)/shard_map/sqhd,skhd->shqk/dot_general | solution.py:204
  394.5 7.0 %multiply_convert_fusion = bf16[3,4,512,512]{2,3,1,0:T(8,128)(2,1)S(1)} fusion(f32[3,4,512,512]{2,3,1,0:T(8,128)} %get-tuple-element.75, f32[3,4,512,512]{2,3,1,0:T(8,128)S(1)} %bitcast.131, f32[3,4,512]{2,1,0:T(4,128)S(1)} %get-tuple-element.74, f32[3,4,512]{2,1,0:T(4,128)S(1)} %log_add_fusion, pred[3,512,512]{1,2,0:T(8,128)(4,1)S(1)} %or_and_fusion), kind=kLoop, calls=%fused_computation | loop fusion | flops 18874368 | bytes 32292864 | tf_op jit(solution)/shard_map/convert_element_type | solution.py:208
  422.4 3.8 reshape.157
  426.2 6.2 %bitcast_convert_fusion = bf16[1536,1024]{1,0:T(8,128)(2,1)} fusion(bf16[3,1024,256]{2,1,0:T(8,128)(2,1)} %param.20, bf16[1,1536,256]{2,1,0:T(8,128)(2,1)S(1)} %copy-done.18, bf16[1,1536,256]{2,1,0:T(8,128)(2,1)} %reshape.158, bf16[1,1536,256]{2,1,0:T(8,128)(2,1)} %reshape.157), kind=kOutput, calls=%fused_computation.9 | convolution fusion | flops 2419851264 | bytes 7077888 | tf_op jit(solution)/shard_map/cte,cde->td/dot_general | solution.py:227
  438.1 39.8 %psum.7 = f32[160,64]{0,1:T(8,128)S(1)} all-reduce(f32[160,64]{0,1:T(8,128)S(1)} %dynamic_update_slice.15), channel_id=1, replica_groups=mesh['dp'=8,'tensor'=4] {'dp','tensor'}, use_global_device_ids=true, to_apply=%region_22.23 | all-reduce | flops 10240 | bytes 81920 | tf_op jit(solution)/shard_map/psum | solution.py:255
  (234 shorter events, 90.7 us)
Async XLA Ops:
  7.2 164.3 %copy-start = (bf16[1024,1024]{1,0:T(8,128)(2,1)S(1)}, bf16[1024,1024]{1,0:T(8,128)(2,1)}, u32[]{:S(2)}) copy-start(bf16[1024,1024]{1,0:T(8,128)(2,1)} %param.22) | copy-start | bytes 6291460
  7.2 33.7 %all-gather.5.cloned.1.call-start = ((), (), s32[]{:S(2)}) async-start(), calls=%async_computation.4 | async-start | bytes 3932160 | tf_op jit(solution)/shard_map/all_gather | solution.py:114
  7.9 130.5 %reduce-scatter.5.cloned.1.call-start = ((), (), s32[]{:S(2)}) async-start(), calls=%async_computation.5 | async-start | bytes 7864320 | tf_op jit(solution)/shard_map/reduce_scatter | solution.py:141
  79.9 61.7 %copy-start.22 = (f32[1024]{0:T(1024)S(1)}, f32[1024]{0:T(1024)}, u32[]{:S(2)}) copy-start(f32[1024]{0:T(1024)} %param.24) | copy-start | bytes 12292
  79.9 91.6 %all-gather.7.cloned.1.call-start = ((), (), s32[]{:S(2)}) async-start(), calls=%async_computation.6 | async-start | bytes 3932160 | tf_op jit(solution)/shard_map/all_gather | solution.py:155
  142.8 93.5 %reduce-scatter.7.cloned.1.call-start = ((), (), s32[]{:S(2)}) async-start(), calls=%async_computation.7 | async-start | bytes 3932160 | tf_op jit(solution)/shard_map/reduce_scatter | solution.py:163
  171.5 21.9 %copy-start.28 = (bf16[1024,1024]{1,0:T(8,128)(2,1)S(1)}, bf16[1024,1024]{1,0:T(8,128)(2,1)}, u32[]{:S(2)}) copy-start(bf16[1024,1024]{1,0:T(8,128)(2,1)} %param.23) | copy-start | bytes 6291460
  198.1 40.6 %copy-start.26 = (f32[1024]{0:T(1024)S(1)}, f32[1024]{0:T(1024)}, u32[]{:S(2)}) copy-start(f32[1024]{0:T(1024)} %param.25) | copy-start | bytes 12292
  198.2 74.8 %all-gather.9.cloned.1.call-start = ((), (), s32[]{:S(2)}) async-start(), calls=%async_computation.8 | async-start | bytes 3932160 | tf_op jit(solution)/shard_map/all_gather | solution.py:176
  244.2 83.7 %reduce-scatter.9.cloned.1.call-start = ((), (), s32[]{:S(2)}) async-start(), calls=%async_computation.9 | async-start | bytes 3932160 | tf_op jit(solution)/shard_map/reduce_scatter | solution.py:183
  289.8 74.2 %all-gather.11.cloned.1.call-start = ((), (), s32[]{:S(2)}) async-start(), calls=%async_computation.10 | async-start | bytes 3932160 | tf_op jit(solution)/shard_map/all_gather | solution.py:197
  335.2 151.0 %reduce-scatter.11.cloned.1.call-start = ((), (), s32[]{:S(2)}) async-start(), calls=%async_computation.11 | async-start | bytes 3932160 | tf_op jit(solution)/shard_map/reduce_scatter | solution.py:226
  374.9 9.7 %copy-start.11 = (bf16[3,512,4,64]{1,0,3,2:T(4,128)(2,1)S(1)}, bf16[3,512,4,64]{1,0,3,2:T(4,128)(2,1)}, u32[]{:S(2)}) copy-start(bf16[3,512,4,64]{1,0,3,2:T(4,128)(2,1)} %copy-done.10) | copy-start | bytes 2359300
  374.9 9.7 %copy-start.13 = (bf16[3,512,4,64]{1,3,2,0:T(8,128)(2,1)S(1)}, bf16[3,512,4,64]{1,3,2,0:T(8,128)(2,1)}, u32[]{:S(2)}) copy-start(bf16[3,512,4,64]{1,3,2,0:T(8,128)(2,1)} %copy.187) | copy-start | bytes 2359300
  374.9 19.5 %slice-start = ((s8[12582912]{0:T(1024)(128)(4,1)}), s8[4194304]{0:T(1024)(128)(4,1)S(1)}, s32[]{:S(2)}) async-start(s8[12582912]{0:T(1024)(128)(4,1)} %bitcast.130), calls=%async_computation.12 | async-start | bytes 8388608
  374.9 19.5 %slice-start.1 = ((s8[12582912]{0:T(1024)(128)(4,1)}), s8[4194304]{0:T(1024)(128)(4,1)S(1)}, s32[]{:S(2)}) async-start(s8[12582912]{0:T(1024)(128)(4,1)} %bitcast.130), calls=%async_computation.13 | async-start | bytes 8388608
  384.6 9.8 %slice-start.2 = ((s8[12582912]{0:T(1024)(128)(4,1)}), s8[4194304]{0:T(1024)(128)(4,1)S(1)}, s32[]{:S(2)}) async-start(s8[12582912]{0:T(1024)(128)(4,1)} %bitcast.130), calls=%async_computation.14 | async-start | bytes 8388608
  394.4 7.0 %copy-start.9 = (bf16[3,512,4,64]{1,0,3,2:T(4,128)(2,1)S(1)}, bf16[3,512,4,64]{1,0,3,2:T(4,128)(2,1)}, u32[]{:S(2)}) copy-start(bf16[3,512,4,64]{1,0,3,2:T(4,128)(2,1)} %copy-done.8) | copy-start | bytes 2359300
  415.3 10.9 %copy-start.18 = (bf16[1,1536,256]{2,1,0:T(8,128)(2,1)S(1)}, bf16[1,1536,256]{2,1,0:T(8,128)(2,1)}, u32[]{:S(2)}) copy-start(bf16[1,1536,256]{2,1,0:T(8,128)(2,1)} %reshape.159) | copy-start | bytes 2359300
  432.4 46.9 %copy-start.27 = (f32[32,32]{1,0:T(8,128)S(1)}, f32[32,32]{1,0:T(8,128)}, u32[]{:S(2)}) copy-start(f32[32,32]{1,0:T(8,128)} %param.29) | copy-start | bytes 12292
  432.4 47.2 %copy-start.17 = (f32[6,64,64]{2,1,0:T(8,128)S(1)}, f32[6,64,64]{2,1,0:T(8,128)}, u32[]{:S(2)}) copy-start(f32[6,64,64]{2,1,0:T(8,128)} %param.32) | copy-start | bytes 294916
  432.4 47.9 %copy-start.24 = (f32[4,16,16]{2,1,0:T(8,128)S(1)}, f32[4,16,16]{2,1,0:T(8,128)}, u32[]{:S(2)}) copy-start(f32[4,16,16]{2,1,0:T(8,128)} %param.31) | copy-start | bytes 12292
  432.4 51.9 %copy-start.23 = (f32[64,64]{1,0:T(8,128)S(1)}, f32[64,64]{1,0:T(8,128)}, u32[]{:S(2)}) copy-start(f32[64,64]{1,0:T(8,128)} %param.30) | copy-start | bytes 49156
  479.3 9.6 %copy-start.16 = (f32[160,64]{0,1:T(8,128)}, f32[160,64]{0,1:T(8,128)S(1)}, u32[]{:S(2)}) copy-start(f32[160,64]{0,1:T(8,128)S(1)} %broadcast_multiply_fusion) | copy-start | bytes 122884
  (21 other events, 73.1 us)
Sparse Core Ops, SparseCore 0:
  9.6 31.2 all-gather.4
  80.0 58.3 reduce-scatter.4
  142.9 28.5 all-gather.6
  198.3 37.9 reduce-scatter.6
  244.4 28.5 all-gather.8
  289.9 37.9 reduce-scatter.8
  335.4 28.5 all-gather.10
  432.6 38.1 reduce-scatter.10

commit v2 on v1

v2 whole, which is shorter than its diff:
```python
from functools import partial

import jax
import jax.numpy as jnp
from jax import lax
from jax.experimental import pallas as pl
from jax.experimental.pallas import tpu as pltpu
from jax.sharding import PartitionSpec as P

D = 1024
HEADS = 16
HD = 64
PAIR = 2 * HD
SEQ = 512
STEP = 10
FR = 64
DR = 16
BROWS = 160
AT_QUERY, AT_VALUE, AT_HIDDEN = 0, D, 2 * D
AT_OUT = 2 * D + FR * HD
AT_FIRST, AT_FFN, AT_SECOND = AT_OUT + D, AT_OUT + 2 * D, AT_OUT + 3 * D
FLAT = BROWS * HD

EPS_NORM = 1e-12
CLIP_LIMIT = 64.0
BETA_ONE = 0.9
BETA_TWO = 0.99
ADAM_EPS = 1e-08
LEARN_RATE = 0.2
HIGHEST = lax.Precision.HIGHEST
MESH_ID = pl.DeviceIdType.MESH
BF16 = jnp.bfloat16
F32 = jnp.float32

SUBS = 4
UNIT = 256
TILE = 256


def nn(a, b):
    return jnp.dot(a, b, preferred_element_type=F32)


def nt(a, b):
    return lax.dot_general(a, b, (((1,), (1,)), ((), ())), preferred_element_type=F32)


def tn(a, b):
    return lax.dot_general(a, b, (((0,), (0,)), ((), ())), preferred_element_type=F32)


def flip(value, bit):
    return value + bit - 2 * bit * ((value // bit) % 2)


class Layout:
    def __init__(self, dp_size, ranks, tokens):
        self.dp_size, self.ranks, self.tokens = dp_size, ranks, tokens
        self.block = 1
        while tokens % (2 * self.block) == 0 and SEQ % (2 * self.block) == 0:
            self.block *= 2
        self.blocks = tokens // self.block
        self.units = SEQ // self.block
        self.width = D // ranks
        self.pairs = self.width // PAIR
        self.hidden = FR * HD // ranks
        rows = ranks * tokens // SEQ
        self.span = 1
        for row in range(rows):
            first = row * self.units // self.blocks
            last = (row * self.units + self.units - 1) // self.blocks
            self.span = max(self.span, last - first + 1)
        self.quads = ranks == 4 and dp_size % 4 == 0
        self.stages = [("tensor", 1 << b) for b in range(ranks.bit_length() - 1)]
        self.stages += [("dp", 1 << b) for b in range(dp_size.bit_length() - 1)]


def layer_kernel(
    lay,
    x,
    og,
    gain1,
    gain2,
    brow,
    seg,
    val,
    wqkv_in,
    wo_in,
    w1_in,
    w2_in,
    out,
    ig,
    bsum,
    wqkv,
    wo_b,
    w1_b,
    w2_b,
    xkv,
    qbuf,
    kbuf,
    vbuf,
    pbuf,
    linv,
    mask,
    ctx,
    cgrad,
    abuf,
    bbuf,
    cbuf,
    r1buf,
    low,
    hid,
    gp,
    back,
    dka,
    dva,
    arecv,
    sem_local,
    sem_own_s,
    sem_own_r,
    sem_y,
    sem_x,
    sem_z,
    sem_c,
    sem_w,
    sem_p,
    sem_hs,
    sem_hr,
    sem_gs,
    sem_gr,
    sem_as,
    sem_ar,
):
    T, S, B, NB, NU = lay.ranks, lay.tokens, lay.block, lay.blocks, lay.units
    W, PP, F = lay.width, lay.pairs, lay.hidden
    dp = lax.axis_index("dp")
    t = lax.axis_index("tensor")
    quads = lay.quads

    def rank(o):
        r = (t + o) % 2
        if T > 2:
            r = r + 2 * ((t // 2 + o // 2) % 2)
        if T > 4:
            r = r + 4 * ((t // 4 + o // 4) % 2)
        return r

    if quads:
        big = wo_b

        def wo(r):
            return big.at[r, pl.ds(0, W)]

        def w1(r):
            return big.at[r, pl.ds(W, D)]

        def w2(r):
            return big.at[r, pl.ds(W + D, F)]
    else:

        def wo(r):
            return wo_b.at[r]

        def w1(r):
            return w1_b.at[r]

        def w2(r):
            return w2_b.at[r]

    def pieces(r):
        return [wqkv.at[r], wo(r), w1(r), w2(r)]

    sources = [wqkv_in, wo_in, w1_in, w2_in]

    def peer(o):
        return (dp, rank(o))

    def remote(src, dst, send, recv, device):
        return pltpu.make_async_remote_copy(
            src_ref=src,
            dst_ref=dst,
            send_sem=send,
            recv_sem=recv,
            device_id=device,
            device_id_type=MESH_ID,
        )

    barrier = pltpu.get_barrier_semaphore()
    others = [peer(o) for o in range(1, T)]
    others += [(flip(dp, bit), t) for axis, bit in lay.stages if axis == "dp"]
    for device in others:
        pl.semaphore_signal(barrier, inc=1, device_id=device, device_id_type=MESH_ID)
    local = [
        pltpu.make_async_copy(src, dst, sem_local.at[i])
        for i, (src, dst) in enumerate(zip(sources, pieces(t)))
    ]
    for copy in local:
        copy.start()
    pl.semaphore_wait(barrier, len(others))

    row0 = (NB * t) // NU
    has_b = (NB * t + NB - 1) // NU != row0

    def place(j):
        u = NB * t + j
        row = u // NU
        return u, row, row - row0, u - row * NU

    def rows_at(w):
        return pl.ds(pl.multiple_of(w * B, B), B)

    def block_at(j):
        return pl.ds(j * B, B)

    for j in range(NB):
        u, row, slot, w = place(j)
        first = row * NU // NB
        last = (row * NU + NU - 1) // NB
        for o in range(lay.span):
            dest = first + o

            @pl.when((dest <= last) & (dest != t))
            def _():
                remote(
                    x.at[block_at(j)],
                    xkv.at[row - (NB * dest) // NU, rows_at(w)],
                    sem_hs.at[j * lay.span + o],
                    sem_hr.at[(row - (NB * dest) // NU) * NU + w],
                    (dp, dest),
                ).start()

    if quads:
        role = dp % 4
        relay = role == 3
        gy = role % 3
        gx = jnp.where(role == 1, 0, jnp.where(role == 3, 2, 1))
        gz = jnp.where(role == 2, 0, jnp.where(role == 3, 1, 2))
        far = rank(2)
        core, ynext = (dp, rank(1)), (dp, rank(2))
        xnext, znext = (flip(dp, 1), t), (flip(dp, 2), t)
        rounds = 4
        steps = rounds * SUBS
        part_a, part_b = D // SUBS, UNIT // SUBS

        def chunk(idx, g, fn):
            n = (idx // SUBS * 3 + g) * SUBS + idx % SUBS

            @pl.when((idx >= 0) & (idx < SUBS))
            def _():
                at = pl.ds(pl.multiple_of(idx * part_a, part_a), part_a)
                fn(lambda r: wqkv.at[r, g, at], n)

            @pl.when((idx >= SUBS) & (idx < steps))
            def _():
                row = ((idx // SUBS - 1) * 3 + g) * UNIT + (idx % SUBS) * part_b
                at = pl.ds(pl.multiple_of(row, part_b), part_b)
                fn(lambda r: big.at[r, at], n)

        def send_y(idx):
            def go(view, n):
                remote(view(t), view(t), sem_y.at[idx], sem_w.at[n], ynext).start()

            chunk(idx, gy, go)

        def to_core(view, n):
            remote(view(far), view(far), sem_c.at[n], sem_p.at[n], core).start()

        def arrived(view, n):
            remote(view(far), view(far), sem_c.at[n], sem_w.at[n], core).wait_recv()

        def to_x(view, n, idx):
            remote(view(far), view(far), sem_x.at[idx], sem_w.at[n], xnext).start()

        def to_z(view, n, idx):
            remote(view(far), view(far), sem_z.at[idx], sem_w.at[n], znext).start()

        def service(s, carry):
            def from_y(view, n):
                arrived(view, n)

                @pl.when(role != 3)
                def _():
                    to_x(view, n, s)
                    to_z(view, n, s)

                to_core(view, n)

            chunk(s, gy, from_y)
            send_y(s + SUBS)
            late = s - jnp.where(relay, 1, 2)

            def from_x(view, n):
                arrived(view, n)

                @pl.when(relay)
                def _():
                    to_z(view, n, late)

                to_core(view, n)

            def from_z(view, n):
                arrived(view, n)

                @pl.when(relay)
                def _():
                    to_x(view, n, late)

                to_core(view, n)

            chunk(late, gx, from_x)
            chunk(late, gz, from_z)
            return carry

        def services(low_step, high_step):
            lax.fori_loop(low_step, high_step, service, 0)

        def sent(idx, carry):
            def go(view, n):
                remote(view(t), view(t), sem_y.at[idx], sem_w.at[n], ynext).wait_send()
                remote(view(t), view(t), sem_x.at[idx], sem_w.at[n], xnext).wait_send()
                remote(view(t), view(t), sem_z.at[idx], sem_w.at[n], znext).wait_send()
                for g in range(3):
                    m = (idx // SUBS * 3 + g) * SUBS + idx % SUBS
                    remote(view(t), view(t), sem_c.at[m], sem_p.at[m], core).wait_send()

            chunk(idx, gy, go)
            return carry

        def from_partner(unit_low, unit_high):
            def go(n, carry):
                @pl.when(n < 3 * SUBS)
                def _():
                    view = wqkv.at[rank(3), 0, pl.ds(0, part_a)]
                    remote(view, view, sem_c.at[n], sem_p.at[n], core).wait_recv()

                @pl.when(n >= 3 * SUBS)
                def _():
                    view = big.at[rank(3), pl.ds(0, part_b)]
                    remote(view, view, sem_c.at[n], sem_p.at[n], core).wait_recv()

                return carry

            lax.fori_loop(unit_low * SUBS, unit_high * SUBS, go, 0)

        def own_copies(i):
            return remote(sources[i], pieces(t)[i], sem_own_s.at[i], sem_own_r.at[i], core)

        local[0].wait()
        lax.fori_loop(0, SUBS, lambda i, c: (send_y(i), c)[1], 0)
        for i in range(4):
            own_copies(i).start()
        for i in range(1, 4):
            local[i].wait()

        def have(i, o):
            if o == 1:
                remote(
                    sources[i], pieces(rank(1))[i], sem_own_s.at[i], sem_own_r.at[i], core
                ).wait_recv()

    else:

        def own_copies(i, o):
            n = i * T + o
            return remote(sources[i], pieces(t)[i], sem_own_s.at[n], sem_own_r.at[n], peer(o))

        for i in range(4):
            for o in range(1, T):
                own_copies(i, o).start()

        def services(low_step, high_step):
            pass

        def have(i, o):
            if o == 0:
                local[i].wait()
            else:
                n = i * T + o
                remote(
                    sources[i], pieces(rank(o))[i], sem_own_s.at[n], sem_own_r.at[n], peer(o)
                ).wait_recv()

    key_at = lax.broadcasted_iota(jnp.int32, (B, SEQ), 1)
    query_at = lax.broadcasted_iota(jnp.int32, (B, SEQ), 0)
    for j in range(NB):
        u, row, slot, w = place(j)
        numbers = seg[pl.ds(row, 1), :].astype(F32)
        keyed = jnp.where(val[pl.ds(row, 1), :] == 1, numbers, -1.0)
        same = key_at == query_at + w * B
        own = jnp.sum(jnp.where(same, numbers, 0.0), axis=1, keepdims=True)
        mask[j] = jnp.where((own == keyed) | same, 0.0, -1e30)
        xkv[slot, rows_at(w)] = x[block_at(j)]

    head_lane = lax.broadcasted_iota(jnp.int32, (B, PAIR), 1) < HD

    def split_heads(values):
        nought = jnp.zeros_like(values)
        return jnp.concatenate(
            [jnp.where(head_lane, values, nought), jnp.where(head_lane, nought, values)], axis=0
        )

    def join_heads(values):
        return jnp.where(head_lane, values[:B], values[B:])

    ones = jnp.ones((SEQ, PAIR), BF16)

    slot_first = jnp.where(has_b & (t % 4 == 2), 1, 0)

    def project_query(r):
        bias = brow[:, pl.ds(pl.multiple_of(AT_QUERY + r * W, PAIR), W)]
        query = ((nn(x[...], wqkv[r, 0]) + bias) * HD**-0.5).astype(BF16)
        for i in range(PP):
            qbuf[r * PP + i] = query[:, i * PAIR : (i + 1) * PAIR]

    def project_keys(r, first_time):
        bias = brow[:, pl.ds(pl.multiple_of(AT_VALUE + r * W, PAIR), W)]

        def body(turn, carry):
            slot = (slot_first + turn) % 2

            @pl.when((slot == 0) | has_b)
            def _():
                if first_time:
                    for w in range(NU):
                        owner = ((row0 + slot) * NU + w) // NB

                        @pl.when(owner != t)
                        def _():
                            remote(
                                x.at[block_at(0)],
                                xkv.at[slot, rows_at(w)],
                                sem_hs.at[0],
                                sem_hr.at[slot * NU + w],
                                (dp, owner),
                            ).wait_recv()

                rows = xkv[slot]
                keys = nn(rows, wqkv[r, 1]).astype(BF16)
                values = (nn(rows, wqkv[r, 2]) + bias).astype(BF16)
                for i in range(PP):
                    kbuf[r * PP + i, slot] = keys[:, i * PAIR : (i + 1) * PAIR]
                    vbuf[r * PP + i, slot] = values[:, i * PAIR : (i + 1) * PAIR]

            return carry

        lax.fori_loop(0, 2, body, 0)

    def attend(r, i):
        hp = r * PP + i
        for j in range(NB):
            u, row, slot, w = place(j)
            query = split_heads(qbuf[hp, block_at(j)])
            hide = mask[j]
            scores = nt(query, kbuf[hp, slot]) + jnp.concatenate([hide, hide], axis=0)
            peak = jnp.max(scores, axis=1, keepdims=True)
            probs = jnp.exp(scores - peak).astype(BF16)
            pbuf[hp, j] = probs
            mixed = nn(probs, jnp.concatenate([vbuf[hp, slot], ones], axis=1))
            inverse = 1.0 / join_heads(mixed[:, PAIR:])
            linv[hp, block_at(j)] = inverse
            ctx[r, block_at(j), pl.ds(i * PAIR, PAIR)] = (
                join_heads(mixed[:, :PAIR]) * inverse
            ).astype(BF16)

    def attention(o, first_time):
        r = rank(o)
        project_query(r)
        project_keys(r, first_time)
        for i in range(PP):
            attend(r, i)

    arrival = [(k + 1) * SUBS + 2 for k in range(4)]
    have(0, 0) if not quads else None
    attention(0, True)
    have(0, 1)
    services(0, 2)
    attention(1, False)
    if quads:
        services(2, arrival[0])
        attention(2, False)
        services(arrival[0], arrival[0] + 2)
        from_partner(0, 3)
        attention(3, False)
        services(arrival[0] + 2, arrival[1])
        have(1, 1)
        from_partner(3, 4)
    else:
        for o in range(2, T):
            have(0, o)
            attention(o, False)
        for o in range(T):
            have(1, o)

    for n in range(0, D, TILE):
        total = nn(ctx[0], wo(0)[:, n : n + TILE])
        for r in range(1, T):
            total = total + nn(ctx[r], wo(r)[:, n : n + TILE])
        at = pl.ds(n, TILE)
        abuf[:, at] = x[:, at].astype(F32) + total + brow[:, AT_OUT + n : AT_OUT + n + TILE]

    def row_mean(values):
        return jnp.mean(values, axis=1, keepdims=True)

    def row_tiles(body, carry):
        for j in range(NB):
            carry = body(block_at(j), carry)
        return carry

    def norm_first(at, carry):
        values = abuf[at]
        centred = values - row_mean(values)
        root = lax.rsqrt(row_mean(centred * centred) + EPS_NORM)
        normed = centred * root
        r1buf[at] = root
        abuf[at] = normed
        low[at] = (normed * gain1[...] + brow[:, AT_FIRST : AT_FIRST + D]).astype(BF16)
        return carry

    row_tiles(norm_first, 0)

    def expand(o):
        r = rank(o)
        for n in range(0, F, TILE):
            bias = brow[:, pl.ds(pl.multiple_of(AT_HIDDEN + r * F + n, PAIR), TILE)]
            pre = nn(low[...], w1(r)[:, n : n + TILE]) + bias
            cdf = 0.5 * (1.0 + lax.erf(pre * 0.5**0.5))
            density = jnp.exp(-0.5 * pre * pre) * 0.3989422804014327
            hid[r, :, pl.ds(n, TILE)] = (pre * cdf).astype(BF16)
            gp[r, :, pl.ds(n, TILE)] = (cdf + pre * density).astype(BF16)

    def reduce(o, start):
        r = rank(o)
        for n in range(0, D, TILE):
            at = pl.ds(n, TILE)
            part = nn(hid[r], w2(r)[:, n : n + TILE])
            bbuf[:, at] = part if start else bbuf[:, at] + part

    have(2, 0) if not quads else None
    expand(0)
    have(2, 1)
    expand(1)
    if quads:
        services(arrival[1], arrival[1] + 2)
        reduce(0, True)
        have(3, 1)
        reduce(1, False)
        services(arrival[1] + 2, arrival[2])
        expand(2)
        from_partner(4, 8)
        expand(3)
        services(arrival[2], arrival[3])
        reduce(2, False)
        from_partner(8, 12)
        reduce(3, False)
    else:
        for o in range(2, T):
            have(2, o)
            expand(o)
        for o in range(T):
            have(3, o)
            reduce(o, o == 0)

    nought_row = jnp.zeros((1, D), F32)

    def norm_second(at, carry):
        sum_up, sum_second = carry
        first_normed = abuf[at] * gain1[...] + brow[:, AT_FIRST : AT_FIRST + D]
        values = first_normed + bbuf[at] + brow[:, AT_FFN : AT_FFN + D]
        centred = values - row_mean(values)
        root = lax.rsqrt(row_mean(centred * centred) + EPS_NORM)
        normed = centred * root
        out[at] = (normed * gain2[...] + brow[:, AT_SECOND : AT_SECOND + D]).astype(BF16)
        upstream = og[at].astype(F32)
        weighted = upstream * gain2[...]
        grad = root * (weighted - row_mean(weighted) - normed * row_mean(weighted * normed))
        bbuf[at] = grad
        low[at] = grad.astype(BF16)
        return (
            sum_up + jnp.sum(upstream, axis=0, keepdims=True),
            sum_second + jnp.sum(grad, axis=0, keepdims=True),
        )

    sum_up, sum_second = row_tiles(norm_second, (nought_row, nought_row))
    bsum[:, AT_SECOND : AT_SECOND + D] = sum_up
    bsum[:, AT_FFN : AT_FFN + D] = sum_second

    def ffn_back(r, carry):
        for n in range(0, F, TILE):
            grad = nt(low[...], w2(r)[n : n + TILE, :]) * gp[r, :, pl.ds(n, TILE)].astype(F32)
            at = pl.ds(pl.multiple_of(AT_HIDDEN + r * F + n, PAIR), TILE)
            bsum[:, at] = jnp.sum(grad, axis=0, keepdims=True)
            hid[r, :, pl.ds(n, TILE)] = grad.astype(BF16)
        return carry

    lax.fori_loop(0, T, ffn_back, 0)
    for n in range(0, D, TILE):
        total = nt(hid[0], w1(0)[n : n + TILE, :])
        for r in range(1, T):
            total = total + nt(hid[r], w1(r)[n : n + TILE, :])
        cbuf[:, pl.ds(n, TILE)] = total

    def first_back(at, carry):
        sum_normed, sum_first = carry
        grad = bbuf[at] + cbuf[at]
        normed = abuf[at]
        weighted = grad * gain1[...]
        first = r1buf[at] * (
            weighted - row_mean(weighted) - normed * row_mean(weighted * normed)
        )
        bbuf[at] = first
        low[at] = first.astype(BF16)
        return (
            sum_normed + jnp.sum(grad, axis=0, keepdims=True),
            sum_first + jnp.sum(first, axis=0, keepdims=True),
        )

    sum_normed, sum_first = row_tiles(first_back, (nought_row, nought_row))
    bsum[:, AT_FIRST : AT_FIRST + D] = sum_normed
    bsum[:, AT_OUT : AT_OUT + D] = sum_first

    for r in range(T):
        cgrad[r] = nt(low[...], wo(r)[...]).astype(BF16)

    def attend_back(r, i):
        hp = r * PP + i
        dka[...] = jnp.zeros_like(dka)
        dva[...] = jnp.zeros_like(dva)
        query_sum = jnp.zeros((1, PAIR), F32)
        for j in range(NB):
            u, row, slot, w = place(j)
            lanes = pl.ds(i * PAIR, PAIR)
            scaled = cgrad[r, block_at(j), lanes].astype(F32) * linv[hp, block_at(j)]
            upstream = split_heads(scaled.astype(BF16))
            delta = jnp.sum(
                split_heads(scaled * ctx[r, block_at(j), lanes].astype(F32)), axis=1, keepdims=True
            )
            probs = pbuf[hp, j]
            query = split_heads(qbuf[hp, block_at(j)])
            score = (probs.astype(F32) * (nt(upstream, vbuf[hp, slot]) - delta)).astype(BF16)
            dva[slot] += tn(probs, upstream)
            dka[slot] += tn(score, query)
            grad = join_heads(nn(score, kbuf[hp, slot])) * HD**-0.5
            qbuf[hp, block_at(j)] = grad.astype(BF16)
            query_sum = query_sum + jnp.sum(grad, axis=0, keepdims=True)
        value_sum = jnp.zeros((1, PAIR), F32)
        for slot in range(2):
            kbuf[hp, slot] = dka[slot].astype(BF16)
            vbuf[hp, slot] = dva[slot].astype(BF16)
            value_sum = value_sum + jnp.sum(dva[slot], axis=0, keepdims=True)
        lanes = pl.multiple_of(r * W + i * PAIR, PAIR)
        bsum[:, pl.ds(AT_QUERY + lanes, PAIR)] = query_sum
        bsum[:, pl.ds(AT_VALUE + lanes, PAIR)] = value_sum

    def rank_back(r, carry):
        for i in range(PP):
            attend_back(r, i)
        return carry

    lax.fori_loop(0, T, rank_back, 0)

    def stage_copy(i):
        axis, bit = lay.stages[i]
        device = (dp, flip(t, bit)) if axis == "tensor" else (flip(dp, bit), t)
        return remote(bsum, arecv.at[i], sem_as.at[i], sem_ar.at[i], device)

    def stage_end(i):
        stage_copy(i).wait()
        bsum[...] = bsum[...] + arecv[i]

    stage_copy(0).start()

    def wide(buffer, r, *at):
        return jnp.concatenate([buffer[(r * PP + i, *at)] for i in range(PP)], axis=1)

    def shares(slot):
        def body(k, carry):
            at = pl.ds(pl.multiple_of(k * TILE, TILE), TILE)
            total = nt(wide(kbuf, 0, slot), wqkv[0, 1, at])
            total = total + nt(wide(vbuf, 0, slot), wqkv[0, 2, at])
            for r in range(1, T):
                total = total + nt(wide(kbuf, r, slot), wqkv[r, 1, at])
                total = total + nt(wide(vbuf, r, slot), wqkv[r, 2, at])
            xkv[slot, :, at] = total.astype(BF16)
            return carry

        lax.fori_loop(0, D // TILE, body, 0)

    def share_copy(slot, w):
        u = (row0 + slot) * NU + w
        owner = u // NB
        first = (row0 + slot) * NU // NB
        place_of = t - first - jnp.where(t > owner, 1, 0)
        number = (u - owner * NB) * (lay.span - 1) + place_of
        return remote(
            xkv.at[slot, rows_at(w)],
            back.at[number],
            sem_gs.at[slot * NU + w],
            sem_gr.at[number],
            (dp, owner),
        )

    def send_shares(turn, carry):
        slot = (1 - slot_first + turn) % 2

        @pl.when((slot == 0) | has_b)
        def _():
            shares(slot)
            for w in range(NU):
                owner = ((row0 + slot) * NU + w) // NB

                @pl.when(owner != t)
                def _():
                    share_copy(slot, w).start()

        return carry

    lax.fori_loop(0, 2, send_shares, 0)
    stage_end(0)
    if len(lay.stages) > 1:
        stage_copy(1).start()

    for n in range(0, D, TILE):
        total = nt(wide(qbuf, 0), wqkv[0, 0, pl.ds(n, TILE)])
        for r in range(1, T):
            total = total + nt(wide(qbuf, r), wqkv[r, 0, pl.ds(n, TILE)])
        at = pl.ds(n, TILE)
        bbuf[:, at] = bbuf[:, at] + total

    for i in range(1, len(lay.stages)):
        stage_end(i)
        if i + 1 < len(lay.stages):
            stage_copy(i + 1).start()

    for j in range(NB):
        u, row, slot, w = place(j)
        first = row * NU // NB
        last = (row * NU + NU - 1) // NB
        bbuf[block_at(j)] = bbuf[block_at(j)] + xkv[slot, rows_at(w)].astype(F32)
        for o in range(lay.span - 1):
            number = j * (lay.span - 1) + o

            @pl.when(first + o < last)
            def _():
                sender = first + o + jnp.where(first + o >= t, 1, 0)
                remote(
                    xkv.at[0, rows_at(0)],
                    back.at[number],
                    sem_gs.at[0],
                    sem_gr.at[number],
                    (dp, sender),
                ).wait_recv()
                bbuf[block_at(j)] = bbuf[block_at(j)] + back[number].astype(F32)

        ig[block_at(j)] = bbuf[block_at(j)].astype(BF16)

    for slot in range(2):
        for w in range(NU):
            owner = ((row0 + slot) * NU + w) // NB

            @pl.when((owner != t) & ((slot == 0) | has_b))
            def _():
                share_copy(slot, w).wait_send()

    for j in range(NB):
        u, row, slot, w = place(j)
        first = row * NU // NB
        last = (row * NU + NU - 1) // NB
        for o in range(lay.span):
            dest = first + o

            @pl.when((dest <= last) & (dest != t))
            def _():
                remote(
                    x.at[block_at(j)],
                    xkv.at[0, rows_at(0)],
                    sem_hs.at[j * lay.span + o],
                    sem_hr.at[0],
                    (dp, dest),
                ).wait_send()

    if quads:
        for i in range(4):
            own_copies(i).wait_send()
        lax.fori_loop(0, steps, sent, 0)
    else:
        for i in range(4):
            for o in range(1, T):
                own_copies(i, o).wait_send()


def layer_call(lay, *args):
    T, S = lay.ranks, lay.tokens
    hp = HEADS // 2
    vmem = pltpu.VMEM
    if lay.quads:
        wide = [
            vmem((T, lay.width + D + lay.hidden, D), BF16),
            vmem((16, PAIR), BF16),
            vmem((16, PAIR), BF16),
        ]
    else:
        wide = [
            vmem((T, lay.width, D), BF16),
            vmem((T, D, lay.hidden), BF16),
            vmem((T, lay.hidden, D), BF16),
        ]
    dma = pltpu.SemaphoreType.DMA
    steps = 4 * SUBS
    own = 4 if lay.quads else 4 * T
    stages = len(lay.stages)
    sharers = lay.blocks * max(lay.span - 1, 1)
    scratch = (
        [vmem((T, 3, D, lay.width), BF16)]
        + wide
        + [
            vmem((2, SEQ, D), BF16),
            vmem((hp, S, PAIR), BF16),
            vmem((hp, 2, SEQ, PAIR), BF16),
            vmem((hp, 2, SEQ, PAIR), BF16),
            vmem((hp, lay.blocks, 2 * lay.block, SEQ), BF16),
            vmem((hp, S, PAIR), F32),
            vmem((lay.blocks, lay.block, SEQ), F32),
            vmem((T, S, lay.width), BF16),
            vmem((T, S, lay.width), BF16),
            vmem((S, D), F32),
            vmem((S, D), F32),
            vmem((S, D), F32),
            vmem((S, 1), F32),
            vmem((S, D), BF16),
            vmem((T, S, lay.hidden), BF16),
            vmem((T, S, lay.hidden), BF16),
            vmem((sharers, lay.block, D), BF16),
            vmem((2, SEQ, PAIR), F32),
            vmem((2, SEQ, PAIR), F32),
            vmem((stages, 1, FLAT), F32),
            dma((4,)),
            dma((own,)),
            dma((own,)),
            dma((steps,)),
            dma((steps,)),
            dma((steps,)),
            dma((3 * steps,)),
            dma((3 * steps,)),
            dma((3 * steps,)),
            dma((lay.blocks * lay.span,)),
            dma((2 * lay.units,)),
            dma((2 * lay.units,)),
            dma((sharers,)),
            dma((stages,)),
            dma((stages,)),
        ]
    )
    in_vmem = pl.BlockSpec(memory_space=pltpu.VMEM)
    anywhere = pl.BlockSpec(memory_space=pl.ANY)
    return pl.pallas_call(
        partial(layer_kernel, lay),
        out_shape=(
            jax.ShapeDtypeStruct((S, D), BF16),
            jax.ShapeDtypeStruct((S, D), BF16),
            jax.ShapeDtypeStruct((1, FLAT), F32),
        ),
        in_specs=[in_vmem] * 7 + [anywhere] * 4,
        out_specs=(in_vmem,) * 3,
        scratch_shapes=scratch,
        compiler_params=pltpu.CompilerParams(
            collective_id=0, has_side_effects=True, vmem_limit_bytes=VMEM_BYTES
        ),
        name="layer",
    )(*args)


VMEM_BYTES = 63 * 2**20


def update_kernel(
    raw,
    biases,
    moment_one,
    moment_two,
    left_pairs,
    left_hidden,
    left_small,
    right_bases,
    owners,
    clipped_out,
    norm_out,
    new_out,
    copies_out,
    one_out,
    two_out,
):
    sums = raw[...]
    norm = jnp.sqrt(jnp.sum(sums * sums, keepdims=True))
    norm_out[...] = norm
    clipped = sums * (CLIP_LIMIT / jnp.maximum(norm, CLIP_LIMIT))
    clipped_out[...] = clipped
    dp = lax.axis_index("dp")
    tail = 2 * HEADS + FR
    layout = [(0, 2 * HEADS, left_pairs), (2 * HEADS, FR, left_hidden)]
    layout += [(tail + k * DR, DR, left_small.at[k]) for k in range(4)]
    for k, (begin, amount, left) in enumerate(layout):
        at = pl.ds(begin, amount)
        right = right_bases[k]
        half = lax.dot_general(
            left[...],
            clipped[begin : begin + amount],
            (((0,), (0,)), ((), ())),
            precision=HIGHEST,
            preferred_element_type=F32,
        )
        rotated = jnp.dot(half, right, precision=HIGHEST, preferred_element_type=F32)
        one = BETA_ONE * moment_one[at] + (1.0 - BETA_ONE) * rotated
        two = BETA_TWO * moment_two[at] + (1.0 - BETA_TWO) * rotated * rotated
        direction = (
            one / (1.0 - BETA_ONE**STEP) / (jnp.sqrt(two / (1.0 - BETA_TWO**STEP)) + ADAM_EPS)
        )
        half = jnp.dot(left[...], direction, precision=HIGHEST, preferred_element_type=F32)
        turned = lax.dot_general(
            half,
            right,
            (((1,), (1,)), ((), ())),
            precision=HIGHEST,
            preferred_element_type=F32,
        )
        new = biases[at] - LEARN_RATE * turned
        copies_out[at] = new.astype(BF16)
        mine = owners[k] == dp
        new_out[at] = jnp.where(mine, new, 0.0)
        one_out[at] = jnp.where(mine, one, 0.0)
        two_out[at] = jnp.where(mine, two, 0.0)


def update_call(*args):
    in_vmem = pl.BlockSpec(memory_space=pltpu.VMEM)
    block = jax.ShapeDtypeStruct((BROWS, HD), F32)
    return pl.pallas_call(
        update_kernel,
        out_shape=(
            block,
            jax.ShapeDtypeStruct((1, 1), F32),
            block,
            jax.ShapeDtypeStruct((BROWS, HD), BF16),
            block,
            block,
        ),
        in_specs=[in_vmem] * 8 + [pl.BlockSpec(memory_space=pltpu.SMEM)],
        out_specs=(in_vmem,) * 6,
        name="update",
    )(*args)


def on_device(
    dp_size,
    ranks,
    inputs,
    output_grad,
    input_project,
    output_project,
    expand_weight,
    reduce_weight,
    first_gain,
    second_gain,
    biases,
    first_moment,
    second_moment,
    left_pairs,
    left_hidden,
    left_small,
    right_bases,
    segment_number,
    token_mask,
    owners,
):
    lay = Layout(dp_size, ranks, inputs.shape[0])
    layer_out, input_grad, sums = layer_call(
        lay,
        inputs,
        output_grad,
        first_gain.reshape(1, D),
        second_gain.reshape(1, D),
        biases.reshape(1, FLAT),
        segment_number.reshape(-1, SEQ),
        token_mask.reshape(-1, SEQ),
        input_project,
        output_project,
        expand_weight,
        reduce_weight,
    )
    clipped, clip_norm, new_owned, copies, first_owned, second_owned = update_call(
        sums.reshape(BROWS, HD),
        biases,
        first_moment,
        second_moment,
        left_pairs,
        left_hidden,
        left_small,
        right_bases,
        owners,
    )
    return (
        layer_out,
        input_grad,
        clipped,
        clip_norm.reshape(1),
        new_owned,
        copies,
        first_owned,
        second_owned,
    )


def solution(mesh):
    return jax.shard_map(
        partial(on_device, mesh.shape["dp"], mesh.shape["tensor"]),
        mesh=mesh,
        in_specs=(
            P(("dp", "tensor"), None),
            P(("dp", "tensor"), None),
            P(None, None, "tensor"),
            P("tensor", None),
            P(None, "tensor"),
            P("tensor", None),
            P(),
            P(),
            P(),
            P(),
            P(),
            P(),
            P(),
            P(),
            P(),
            P("dp"),
            P("dp"),
            P(),
        ),
        out_specs=(
            P(("dp", "tensor"), None),
            P(("dp", "tensor"), None),
            P(),
            P(),
            P("dp", None),
            P(),
            P("dp", None),
            P("dp", None),
        ),
        check_vma=False,
    )
```

time: 507 us -> 162 us (0.32); the launches traced: 497 us -> 161 us
  waiting for transfers between devices: 243 us -> 0 us
  Pallas kernels: 0 us -> 142 us
  matrix products: 94.3 us -> 0 us
  local copies, waits for them, and re-layouts: 61.8 us -> 16.6 us
  blocking collectives: 39.8 us -> 0 us
  other arithmetic: 37.4 us -> 1.52 us
  between operations: 21 us -> 0.69 us
    pallas_call x0 -> x2, Pallas kernels: none -> 142 us  [the longest x1 138 us: layer_call(): pl.pallas_call(partial(layer_kernel, lay), out_shape=(jax.ShapeDtypeStruc...]
    reduce_scatter x4 -> x0, waiting for transfers between devices: 133 us -> none  [the longest x1 57.3 us: on_device(): lax.psum_scatter(jnp.dot(portion, output_project, preferred_element_type=...]
    all_gather x4 -> x0, waiting for transfers between devices: 108 us -> none  [the longest x1 29.4 us: on_device(): full_inputs = lax.all_gather(inputs, 'tensor', axis=0, tiled=True)]
    dot_general x38 -> x0, matrix products: 94.3 us -> none  [the longest x1 17.4 us: on_device(): jnp.dot(lax.all_gather(normed_low, 'tensor', axis=0, tiled=True), expand_...]
    psum x1 -> x0, blocking collectives: 39.8 us -> none  [on_device(): bias_total = lax.psum(bias_term, ('dp', 'tensor'))]
    reduce_sum x12 -> x0, other arithmetic: 20.4 us -> none  [the longest x4 7.73 us: layer_norm(): centred = values - jnp.mean(values, axis=-1, keepdims=True)]
    another operation x6 -> x0, local copies, waits for them, and re-layouts: 20.2 us -> none  [on_device(): jnp.stack([query_grad, key_grad, value_grad])]
    convert_element_type x7 -> x0, other arithmetic: 15.2 us -> none  [the longest x1 6.97 us: on_device(): score_grad = (probs * (prob_grad - row_delta)).astype(jnp.bfloat16)]
  transfers between devices with their start and end apart: 8 -> 0, of which waited for: 7 -> 0; matrix products, arithmetic and copies ran while one was open for 4% -> 0% of each run, Pallas kernels for 0% -> 0%
where the time goes in v2:
time: 162 us; the launch traced here: 161 us
  Pallas kernels  142 us (88%)
  local copies, waits for them, and re-layouts  16.6 us (10%)
    pallas_call x1, Pallas kernels, layer_call(): pl.pallas_call(partial(layer_kernel, lay), out_shape=(jax.ShapeDtypeStruc...  138 us
    unnamed x20, local copies, waits for them, and re-layouts  12 us
    pallas_call x1, Pallas kernels, update_call(): pl.pallas_call(update_kernel, out_shape=(block, jax.ShapeDtypeStruct((1,...  4.35 us

profile of v2, /device:TPU:0, one launch (start us, length us, event | category | flops | bytes accessed | tf_op | source)
XLA Modules:
  0.0 161.0 jit_solution(17135169878743093331)
XLA Ops:
  0.6 0.9 copy.35.biases
  1.6 0.0 copy-start.2
  1.6 0.7 reshape.39.brow
  2.3 1.3 reshape.40.seg
  3.6 1.3 reshape.41.val
  4.9 137.8 %layer.1 = (bf16[384,1024]{1,0:T(8,128)(2,1)}, bf16[384,1024]{1,0:T(8,128)(2,1)}, f32[1,10240]{1,0:T(1,128)}) custom-call(bf16[384,1024]{1,0:T(8,128)(2,1)} %x.1, bf16[384,1024]{1,0:T(8,128)(2,1)} %og.1, f32[1,1024]{1,0:T(1,128)} %bitcast.3, f32[1,1024]{1,0:T(1,128)} %bitcast.4, f32[1,10240]{1,0:T(1,128)} %reshape.39.brow, s32[3,512]{1,0:T(4,128)} %reshape.40.seg, ...), custom_call_target="tpu_custom_call" | custom-call | tf_op jit(solution)/shard_map/layer/pallas_call | solution.py:855
  142.7 0.0 copy-done.2
  142.8 0.0 copy-start.1
  142.8 0.0 copy-start
  142.8 0.5 broadcast.3
  143.3 1.5 reduce.3
  144.8 0.7 reshape.42.raw
  145.5 0.0 copy-done.3
  145.5 0.7 copy.37.moment_one
  146.3 0.7 copy.38.moment_two
  147.0 4.3 %update.1 = (f32[160,64]{1,0:T(8,128)}, f32[1,1]{1,0:T(1,128)}, f32[160,64]{1,0:T(8,128)}, bf16[160,64]{1,0:T(8,128)(2,1)}, f32[160,64]{1,0:T(8,128)}, /*index=5*/f32[160,64]{1,0:T(8,128)}) custom-call(f32[160,64]{1,0:T(8,128)} %reshape.42.raw, f32[160,64]{1,0:T(8,128)} %copy-done.2, f32[160,64]{1,0:T(8,128)} %copy.37.moment_one, ...), custom_call_target="tpu_custom_call" | custom-call | tf_op jit(solution)/shard_map/update/pallas_call | solution.py:936
  151.3 1.6 copy.39
  152.9 1.6 copy.40
  154.5 1.5 copy.41
  156.0 1.6 copy.42
  157.6 1.6 copy.43
  159.2 0.9 copy.46
  160.1 0.0 copy-done
  160.1 0.9 copy.47
  (4 shorter events, 0.0 us)
Async XLA Ops:
  1.6 141.2 %copy-start.2 = (f32[160,64]{1,0:T(8,128)}, f32[160,64]{1,0:T(8,128)S(1)}, u32[]{:S(2)}) copy-start(f32[160,64]{1,0:T(8,128)S(1)} %copy.35.biases) | copy-start | bytes 122884
  4.9 140.6 %copy-start.3 = (f32[160,64]{0,1:T(8,128)S(1)}, f32[160,64]{0,1:T(8,128)}, u32[]{:S(2)}) copy-start(f32[160,64]{0,1:T(8,128)} %param.27) | copy-start | bytes 122884
  4.9 141.3 %copy-start.4 = (f32[160,64]{0,1:T(8,128)S(1)}, f32[160,64]{0,1:T(8,128)}, u32[]{:S(2)}) copy-start(f32[160,64]{0,1:T(8,128)} %param.28) | copy-start | bytes 122884
  142.8 16.5 %copy-start.1 = (bf16[384,1024]{1,0:T(8,128)(2,1)S(1)}, bf16[384,1024]{1,0:T(8,128)(2,1)}, u32[]{:S(2)}) copy-start(bf16[384,1024]{1,0:T(8,128)(2,1)} %get-tuple-element.50) | copy-start | bytes 2359300
  142.8 17.3 %copy-start = (bf16[384,1024]{1,0:T(8,128)(2,1)S(1)}, bf16[384,1024]{1,0:T(8,128)(2,1)}, u32[]{:S(2)}) copy-start(bf16[384,1024]{1,0:T(8,128)(2,1)} %get-tuple-element.51) | copy-start | bytes 2359300

commit v3 on v2

--- a/solution.py
+++ b/solution.py
@@ -33,6 +33,7 @@
 F32 = jnp.float32
 
 SUBS = 4
+RELAY_LAG, LAG = 2, 4
 UNIT = 256
 TILE = 256
 
@@ -71,8 +72,6 @@
             last = (row * self.units + self.units - 1) // self.blocks
             self.span = max(self.span, last - first + 1)
         self.quads = ranks == 4 and dp_size % 4 == 0
-        self.stages = [("tensor", 1 << b) for b in range(ranks.bit_length() - 1)]
-        self.stages += [("dp", 1 << b) for b in range(dp_size.bit_length() - 1)]
 
 
 def layer_kernel(
@@ -81,16 +80,19 @@
     og,
     gain1,
     gain2,
-    brow,
+    biases_t,
     seg,
     val,
     wqkv_in,
     wo_in,
     w1_in,
     w2_in,
+    out_hbm,
+    ig_hbm,
+    bsum,
+    brow,
     out,
     ig,
-    bsum,
     wqkv,
     wo_b,
     w1_b,
@@ -114,8 +116,12 @@
     back,
     dka,
     dva,
-    arecv,
+    group_early,
+    group_late,
+    all_early,
+    all_late,
     sem_local,
+    sem_out,
     sem_own_s,
     sem_own_r,
     sem_y,
@@ -130,6 +136,8 @@
     sem_gr,
     sem_as,
     sem_ar,
+    sem_bs,
+    sem_br,
 ):
     T, S, B, NB, NU = lay.ranks, lay.tokens, lay.block, lay.blocks, lay.units
     W, PP, F = lay.width, lay.pairs, lay.hidden
@@ -187,7 +195,7 @@
 
     barrier = pltpu.get_barrier_semaphore()
     others = [peer(o) for o in range(1, T)]
-    others += [(flip(dp, bit), t) for axis, bit in lay.stages if axis == "dp"]
+    others += [((dp + o) % lay.dp_size, t) for o in range(1, lay.dp_size)]
     for device in others:
         pl.semaphore_signal(barrier, inc=1, device_id=device, device_id_type=MESH_ID)
     local = [
@@ -196,7 +204,6 @@
     ]
     for copy in local:
         copy.start()
-    pl.semaphore_wait(barrier, len(others))
 
     row0 = (NB * t) // NU
     has_b = (NB * t + NB - 1) // NU != row0
@@ -212,22 +219,41 @@
     def block_at(j):
         return pl.ds(j * B, B)
 
+    key_at = lax.broadcasted_iota(jnp.int32, (B, SEQ), 1)
+    query_at = lax.broadcasted_iota(jnp.int32, (B, SEQ), 0)
     for j in range(NB):
         u, row, slot, w = place(j)
-        first = row * NU // NB
-        last = (row * NU + NU - 1) // NB
-        for o in range(lay.span):
-            dest = first + o
-
-            @pl.when((dest <= last) & (dest != t))
-            def _():
-                remote(
-                    x.at[block_at(j)],
-                    xkv.at[row - (NB * dest) // NU, rows_at(w)],
-                    sem_hs.at[j * lay.span + o],
-                    sem_hr.at[(row - (NB * dest) // NU) * NU + w],
-                    (dp, dest),
-                ).start()
+        keys_here = pl.ds(pl.multiple_of(row * SEQ, SEQ), SEQ)
+        numbers = seg[:, keys_here].astype(F32)
+        keyed = jnp.where(val[:, keys_here] == 1, numbers, -1.0)
+        same = key_at == query_at + w * B
+        own = jnp.sum(jnp.where(same, numbers, 0.0), axis=1, keepdims=True)
+        mask[j] = jnp.where((own == keyed) | same, 0.0, -1e30)
+        xkv[slot, rows_at(w)] = x[block_at(j)]
+
+    bias_rows = biases_t[...].T
+    for i in range(BROWS):
+        brow[:, i * HD : (i + 1) * HD] = bias_rows[i : i + 1]
+
+    pl.semaphore_wait(barrier, len(others))
+
+    def send_rows():
+        for j in range(NB):
+            u, row, slot, w = place(j)
+            first = row * NU // NB
+            last = (row * NU + NU - 1) // NB
+            for o in range(lay.span):
+                dest = first + o
+
+                @pl.when((dest <= last) & (dest != t))
+                def _():
+                    remote(
+                        x.at[block_at(j)],
+                        xkv.at[row - (NB * dest) // NU, rows_at(w)],
+                        sem_hs.at[j * lay.span + o],
+                        sem_hr.at[(row - (NB * dest) // NU) * NU + w],
+                        (dp, dest),
+                    ).start()
 
     if quads:
         role = dp % 4
@@ -287,7 +313,7 @@
 
             chunk(s, gy, from_y)
             send_y(s + SUBS)
-            late = s - jnp.where(relay, 1, 2)
+            late = s - jnp.where(relay, RELAY_LAG, LAG)
 
             def from_x(view, n):
                 arrived(view, n)
@@ -310,9 +336,6 @@
             chunk(late, gx, from_x)
             chunk(late, gz, from_z)
             return carry
-
-        def services(low_step, high_step):
-            lax.fori_loop(low_step, high_step, service, 0)
 
         def sent(idx, carry):
             def go(view, n):
@@ -346,50 +369,49 @@
             return remote(sources[i], pieces(t)[i], sem_own_s.at[i], sem_own_r.at[i], core)
 
         local[0].wait()
-        lax.fori_loop(0, SUBS, lambda i, c: (send_y(i), c)[1], 0)
+        lax.fori_loop(0, 2, lambda i, c: (send_y(i), c)[1], 0)
+        send_rows()
+        lax.fori_loop(2, SUBS, lambda i, c: (send_y(i), c)[1], 0)
         for i in range(4):
             own_copies(i).start()
         for i in range(1, 4):
             local[i].wait()
 
-        def have(i, o):
-            if o == 1:
+        first_unit = [0, 3, 4, 8, 12]
+
+        def ready(i, o):
+            @pl.when(o == 1)
+            def _():
                 remote(
                     sources[i], pieces(rank(1))[i], sem_own_s.at[i], sem_own_r.at[i], core
                 ).wait_recv()
 
+            @pl.when(o == 3)
+            def _():
+                from_partner(first_unit[i], first_unit[i + 1])
+
     else:
 
         def own_copies(i, o):
             n = i * T + o
             return remote(sources[i], pieces(t)[i], sem_own_s.at[n], sem_own_r.at[n], peer(o))
 
+        send_rows()
         for i in range(4):
             for o in range(1, T):
                 own_copies(i, o).start()
 
-        def services(low_step, high_step):
-            pass
-
-        def have(i, o):
-            if o == 0:
+        def ready(i, o):
+            @pl.when(o == 0)
+            def _():
                 local[i].wait()
-            else:
+
+            @pl.when(o != 0)
+            def _():
                 n = i * T + o
                 remote(
                     sources[i], pieces(rank(o))[i], sem_own_s.at[n], sem_own_r.at[n], peer(o)
                 ).wait_recv()
-
-    key_at = lax.broadcasted_iota(jnp.int32, (B, SEQ), 1)
-    query_at = lax.broadcasted_iota(jnp.int32, (B, SEQ), 0)
-    for j in range(NB):
-        u, row, slot, w = place(j)
-        numbers = seg[pl.ds(row, 1), :].astype(F32)
-        keyed = jnp.where(val[pl.ds(row, 1), :] == 1, numbers, -1.0)
-        same = key_at == query_at + w * B
-        own = jnp.sum(jnp.where(same, numbers, 0.0), axis=1, keepdims=True)
-        mask[j] = jnp.where((own == keyed) | same, 0.0, -1e30)
-        xkv[slot, rows_at(w)] = x[block_at(j)]
 
     head_lane = lax.broadcasted_iota(jnp.int32, (B, PAIR), 1) < HD
 
@@ -412,7 +434,7 @@
         for i in range(PP):
             qbuf[r * PP + i] = query[:, i * PAIR : (i + 1) * PAIR]
 
-    def project_keys(r, first_time):
+    def project_keys(o, r):
         bias = brow[:, pl.ds(pl.multiple_of(AT_VALUE + r * W, PAIR), W)]
 
         def body(turn, carry):
@@ -420,19 +442,18 @@
 
             @pl.when((slot == 0) | has_b)
             def _():
-                if first_time:
-                    for w in range(NU):
-                        owner = ((row0 + slot) * NU + w) // NB
-
-                        @pl.when(owner != t)
-                        def _():
-                            remote(
-                                x.at[block_at(0)],
-                                xkv.at[slot, rows_at(w)],
-                                sem_hs.at[0],
-                                sem_hr.at[slot * NU + w],
-                                (dp, owner),
-                            ).wait_recv()
+                for w in range(NU):
+                    owner = ((row0 + slot) * NU + w) // NB
+
+                    @pl.when((owner != t) & (o == 0))
+                    def _():
+                        remote(
+                            x.at[block_at(0)],
+                            xkv.at[slot, rows_at(w)],
+                            sem_hs.at[0],
+                            sem_hr.at[slot * NU + w],
+                            (dp, owner),
+                        ).wait_recv()
 
                 rows = xkv[slot]
                 keys = nn(rows, wqkv[r, 1]).astype(BF16)
@@ -462,41 +483,15 @@
                 join_heads(mixed[:, :PAIR]) * inverse
             ).astype(BF16)
 
-    def attention(o, first_time):
+    def project(o):
+        ready(0, o)
         r = rank(o)
         project_query(r)
-        project_keys(r, first_time)
+        project_keys(o, r)
+
+    def attend_rank(o):
         for i in range(PP):
-            attend(r, i)
-
-    arrival = [(k + 1) * SUBS + 2 for k in range(4)]
-    have(0, 0) if not quads else None
-    attention(0, True)
-    have(0, 1)
-    services(0, 2)
-    attention(1, False)
-    if quads:
-        services(2, arrival[0])
-        attention(2, False)
-        services(arrival[0], arrival[0] + 2)
-        from_partner(0, 3)
-        attention(3, False)
-        services(arrival[0] + 2, arrival[1])
-        have(1, 1)
-        from_partner(3, 4)
-    else:
-        for o in range(2, T):
-            have(0, o)
-            attention(o, False)
-        for o in range(T):
-            have(1, o)
-
-    for n in range(0, D, TILE):
-        total = nn(ctx[0], wo(0)[:, n : n + TILE])
-        for r in range(1, T):
-            total = total + nn(ctx[r], wo(r)[:, n : n + TILE])
-        at = pl.ds(n, TILE)
-        abuf[:, at] = x[:, at].astype(F32) + total + brow[:, AT_OUT + n : AT_OUT + n + TILE]
+            attend(rank(o), i)
 
     def row_mean(values):
         return jnp.mean(values, axis=1, keepdims=True)
@@ -513,12 +508,24 @@
         normed = centred * root
         r1buf[at] = root
         abuf[at] = normed
-        low[at] = (normed * gain1[...] + brow[:, AT_FIRST : AT_FIRST + D]).astype(BF16)
+        first_normed = normed * gain1[...] + brow[:, AT_FIRST : AT_FIRST + D]
+        low[at] = first_normed.astype(BF16)
+        bbuf[at] = first_normed + brow[:, AT_FFN : AT_FFN + D]
         return carry
 
-    row_tiles(norm_first, 0)
+    def finish_attention():
+        for o in range(T):
+            ready(1, o)
+        for n in range(0, D, TILE):
+            total = nn(ctx[0], wo(0)[:, n : n + TILE])
+            for r in range(1, T):
+                total = total + nn(ctx[r], wo(r)[:, n : n + TILE])
+            at = pl.ds(n, TILE)
+            abuf[:, at] = x[:, at].astype(F32) + total + brow[:, AT_OUT + n : AT_OUT + n + TILE]
+        row_tiles(norm_first, 0)
 
     def expand(o):
+        ready(2, o)
         r = rank(o)
         for n in range(0, F, TILE):
             bias = brow[:, pl.ds(pl.multiple_of(AT_HIDDEN + r * F + n, PAIR), TILE)]
@@ -528,44 +535,60 @@
             hid[r, :, pl.ds(n, TILE)] = (pre * cdf).astype(BF16)
             gp[r, :, pl.ds(n, TILE)] = (cdf + pre * density).astype(BF16)
 
-    def reduce(o, start):
+    def reduce(o):
+        ready(3, o)
         r = rank(o)
         for n in range(0, D, TILE):
             at = pl.ds(n, TILE)
-            part = nn(hid[r], w2(r)[:, n : n + TILE])
-            bbuf[:, at] = part if start else bbuf[:, at] + part
-
-    have(2, 0) if not quads else None
-    expand(0)
-    have(2, 1)
-    expand(1)
+            bbuf[:, at] = bbuf[:, at] + nn(hid[r], w2(r)[:, n : n + TILE])
+
     if quads:
-        services(arrival[1], arrival[1] + 2)
-        reduce(0, True)
-        have(3, 1)
-        reduce(1, False)
-        services(arrival[1] + 2, arrival[2])
-        expand(2)
-        from_partner(4, 8)
-        expand(3)
-        services(arrival[2], arrival[3])
-        reduce(2, False)
-        from_partner(8, 12)
-        reduce(3, False)
+        whole = [(k + 1) * SUBS + LAG - 1 for k in range(rounds)]
+        mid = SUBS // 2
+        plan = [
+            (project, [PLAN[0], PLAN[1], whole[0], whole[0] + 2]),
+            (attend_rank, [PLAN[2], PLAN[3], whole[0] + 1, whole[0] + 3]),
+            (expand, [whole[1] + 1, whole[1] + 2, whole[2], whole[2] + 1]),
+            (reduce, [whole[1] + 3, whole[1] + 4, whole[3], whole[3]]),
+        ]
+
+        def step(s, carry):
+            service(s, 0)
+
+            @pl.when(s == whole[1])
+            def _():
+                finish_attention()
+
+            for part, at_steps in plan:
+                o = jnp.int32(-1)
+                for k, at_step in enumerate(at_steps):
+                    if at_step < whole[3]:
+                        o = jnp.where(s == at_step, k, o)
+
+                @pl.when(o >= 0)
+                def _():
+                    part(o)
+
+            return carry
+
+        lax.fori_loop(0, whole[3] + 1, step, 0)
+        lax.fori_loop(2, T, lambda o, c: (reduce(o), c)[1], 0)
     else:
-        for o in range(2, T):
-            have(2, o)
-            expand(o)
-        for o in range(T):
-            have(3, o)
-            reduce(o, o == 0)
+
+        def each_rank(part):
+            lax.fori_loop(0, T, lambda o, c: (part(o), c)[1], 0)
+
+        each_rank(project)
+        each_rank(attend_rank)
+        finish_attention()
+        each_rank(expand)
+        each_rank(reduce)
 
     nought_row = jnp.zeros((1, D), F32)
 
     def norm_second(at, carry):
         sum_up, sum_second = carry
-        first_normed = abuf[at] * gain1[...] + brow[:, AT_FIRST : AT_FIRST + D]
-        values = first_normed + bbuf[at] + brow[:, AT_FFN : AT_FFN + D]
+        values = bbuf[at]
         centred = values - row_mean(values)
         root = lax.rsqrt(row_mean(centred * centred) + EPS_NORM)
         normed = centred * root
@@ -581,6 +604,8 @@
         )
 
     sum_up, sum_second = row_tiles(norm_second, (nought_row, nought_row))
+    out_copy = pltpu.make_async_copy(out, out_hbm, sem_out.at[0])
+    out_copy.start()
     bsum[:, AT_SECOND : AT_SECOND + D] = sum_up
     bsum[:, AT_FFN : AT_FFN + D] = sum_second
 
@@ -617,6 +642,59 @@
     sum_normed, sum_first = row_tiles(first_back, (nought_row, nought_row))
     bsum[:, AT_FIRST : AT_FIRST + D] = sum_normed
     bsum[:, AT_OUT : AT_OUT + D] = sum_first
+
+    class Totals:
+        def __init__(self, number, start, amount, group, everyone):
+            self.number, self.at = number, pl.ds(start, amount)
+            self.group, self.everyone = group, everyone
+
+        def copies(self, buffer, sems, me, peers):
+            send, recv = sems
+            return [
+                remote(
+                    buffer.at[me],
+                    buffer.at[me],
+                    send.at[self.number, k],
+                    recv.at[self.number, me],
+                    device,
+                )
+                for k, device in enumerate(peers)
+            ]
+
+        def gather(self, buffer, sems, me, peers):
+            for copy in self.copies(buffer, sems, me, peers):
+                copy.wait_send()
+            for k in range(buffer.shape[0]):
+
+                @pl.when(k != me)
+                def _():
+                    remote(
+                        buffer.at[k], buffer.at[k], sems[0].at[0, 0], sems[1].at[self.number, k], peers[0]
+                    ).wait_recv()
+
+            total = buffer[0]
+            for k in range(1, buffer.shape[0]):
+                total = total + buffer[k]
+            return total
+
+        def start(self):
+            self.group[t] = bsum[:, self.at]
+            for copy in self.copies(self.group, (sem_as, sem_ar), t, in_group):
+                copy.start()
+
+        def middle(self):
+            self.everyone[dp] = self.gather(self.group, (sem_as, sem_ar), t, in_group)
+            for copy in self.copies(self.everyone, (sem_bs, sem_br), dp, in_dp):
+                copy.start()
+
+        def finish(self):
+            bsum[:, self.at] = self.gather(self.everyone, (sem_bs, sem_br), dp, in_dp)
+
+    in_group = [peer(o) for o in range(1, T)]
+    in_dp = [((dp + o) % lay.dp_size, t) for o in range(1, lay.dp_size)]
+    early = Totals(0, AT_HIDDEN, FLAT - AT_HIDDEN, group_early, all_early)
+    late = Totals(1, AT_QUERY, AT_HIDDEN, group_late, all_late)
+    early.start()
 
     for r in range(T):
         cgrad[r] = nt(low[...], wo(r)[...]).astype(BF16)
@@ -654,20 +732,15 @@
     def rank_back(r, carry):
         for i in range(PP):
             attend_back(r, i)
+
+        @pl.when(r == T // 2 - 1)
+        def _():
+            early.middle()
+
         return carry
 
     lax.fori_loop(0, T, rank_back, 0)
-
-    def stage_copy(i):
-        axis, bit = lay.stages[i]
-        device = (dp, flip(t, bit)) if axis == "tensor" else (flip(dp, bit), t)
-        return remote(bsum, arecv.at[i], sem_as.at[i], sem_ar.at[i], device)
-
-    def stage_end(i):
-        stage_copy(i).wait()
-        bsum[...] = bsum[...] + arecv[i]
-
-    stage_copy(0).start()
+    late.start()
 
     def wide(buffer, r, *at):
         return jnp.concatenate([buffer[(r * PP + i, *at)] for i in range(PP)], axis=1)
@@ -715,9 +788,8 @@
         return carry
 
     lax.fori_loop(0, 2, send_shares, 0)
-    stage_end(0)
-    if len(lay.stages) > 1:
-        stage_copy(1).start()
+    late.middle()
+    early.finish()
 
     for n in range(0, D, TILE):
         total = nt(wide(qbuf, 0), wqkv[0, 0, pl.ds(n, TILE)])
@@ -725,11 +797,6 @@
             total = total + nt(wide(qbuf, r), wqkv[r, 0, pl.ds(n, TILE)])
         at = pl.ds(n, TILE)
         bbuf[:, at] = bbuf[:, at] + total
-
-    for i in range(1, len(lay.stages)):
-        stage_end(i)
-        if i + 1 < len(lay.stages):
-            stage_copy(i + 1).start()
 
     for j in range(NB):
         u, row, slot, w = place(j)
@@ -753,6 +820,12 @@
 
         ig[block_at(j)] = bbuf[block_at(j)].astype(BF16)
 
+    ig_copy = pltpu.make_async_copy(ig, ig_hbm, sem_out.at[1])
+    ig_copy.start()
+    late.finish()
+
+    out_copy.wait()
+    ig_copy.wait()
     for slot in range(2):
         for w in range(NU):
             owner = ((row0 + slot) * NU + w) // NB
@@ -807,10 +880,10 @@
     dma = pltpu.SemaphoreType.DMA
     steps = 4 * SUBS
     own = 4 if lay.quads else 4 * T
-    stages = len(lay.stages)
     sharers = lay.blocks * max(lay.span - 1, 1)
     scratch = (
-        [vmem((T, 3, D, lay.width), BF16)]
+        [vmem((1, FLAT), F32), vmem((S, D), BF16), vmem((S, D), BF16)]
+        + [vmem((T, 3, D, lay.width), BF16)]
         + wide
         + [
             vmem((2, SEQ, D), BF16),
@@ -832,8 +905,12 @@
             vmem((sharers, lay.block, D), BF16),
             vmem((2, SEQ, PAIR), F32),
             vmem((2, SEQ, PAIR), F32),
-            vmem((stages, 1, FLAT), F32),
+            vmem((T, 1, FLAT - AT_HIDDEN), F32),
+            vmem((T, 1, AT_HIDDEN), F32),
+            vmem((lay.dp_size, 1, FLAT - AT_HIDDEN), F32),
+            vmem((lay.dp_size, 1, AT_HIDDEN), F32),
             dma((4,)),
+            dma((2,)),
             dma((own,)),
             dma((own,)),
             dma((steps,)),
@@ -846,8 +923,10 @@
             dma((2 * lay.units,)),
             dma((2 * lay.units,)),
             dma((sharers,)),
-            dma((stages,)),
-            dma((stages,)),
+            dma((2, T)),
+            dma((2, T)),
+            dma((2, lay.dp_size)),
+            dma((2, lay.dp_size)),
         ]
     )
     in_vmem = pl.BlockSpec(memory_space=pltpu.VMEM)
@@ -860,7 +939,7 @@
             jax.ShapeDtypeStruct((1, FLAT), F32),
         ),
         in_specs=[in_vmem] * 7 + [anywhere] * 4,
-        out_specs=(in_vmem,) * 3,
+        out_specs=(anywhere, anywhere, in_vmem),
         scratch_shapes=scratch,
         compiler_params=pltpu.CompilerParams(
             collective_id=0, has_side_effects=True, vmem_limit_bytes=VMEM_BYTES
@@ -870,6 +949,7 @@
 
 
 VMEM_BYTES = 63 * 2**20
+PLAN = [2, 5, 3, 6]
 
 
 def update_kernel(
@@ -882,69 +962,107 @@
     left_small,
     right_bases,
     owners,
+    out_in,
+    ig_in,
     clipped_out,
     norm_out,
     new_out,
     copies_out,
     one_out,
     two_out,
+    out_out,
+    ig_out,
+    rows,
+    left,
+    wide,
+    sems,
 ):
+    fetches = [
+        pltpu.make_async_copy(src, wide.at[i], sems.at[i]) for i, src in enumerate((out_in, ig_in))
+    ]
+    stores = [
+        pltpu.make_async_copy(wide.at[i], dst, sems.at[2 + i])
+        for i, dst in enumerate((out_out, ig_out))
+    ]
+    for fetch in fetches:
+        fetch.start()
     sums = raw[...]
     norm = jnp.sqrt(jnp.sum(sums * sums, keepdims=True))
     norm_out[...] = norm
-    clipped = sums * (CLIP_LIMIT / jnp.maximum(norm, CLIP_LIMIT))
+    for i in range(BROWS):
+        rows[i : i + 1] = sums[:, i * HD : (i + 1) * HD]
+    clipped = rows[...].T * (CLIP_LIMIT / jnp.maximum(norm, CLIP_LIMIT))
     clipped_out[...] = clipped
     dp = lax.axis_index("dp")
     tail = 2 * HEADS + FR
     layout = [(0, 2 * HEADS, left_pairs), (2 * HEADS, FR, left_hidden)]
     layout += [(tail + k * DR, DR, left_small.at[k]) for k in range(4)]
-    for k, (begin, amount, left) in enumerate(layout):
-        at = pl.ds(begin, amount)
-        right = right_bases[k]
-        half = lax.dot_general(
-            left[...],
-            clipped[begin : begin + amount],
-            (((0,), (0,)), ((), ())),
+    left[...] = jnp.zeros_like(left)
+    for begin, amount, basis in layout:
+        left[begin : begin + amount, begin : begin + amount] = basis[...]
+    column = lax.broadcasted_iota(jnp.int32, (HD, BROWS), 1)
+
+    def per_matrix(choose):
+        result = choose(0)
+        for k in range(1, len(layout)):
+            result = jnp.where(column >= layout[k][0], choose(k), result)
+        return result
+
+    def product(a, b, over_a, over_b):
+        return lax.dot_general(
+            a,
+            b,
+            (((over_a,), (over_b,)), ((), ())),
             precision=HIGHEST,
             preferred_element_type=F32,
         )
-        rotated = jnp.dot(half, right, precision=HIGHEST, preferred_element_type=F32)
-        one = BETA_ONE * moment_one[at] + (1.0 - BETA_ONE) * rotated
-        two = BETA_TWO * moment_two[at] + (1.0 - BETA_TWO) * rotated * rotated
-        direction = (
-            one / (1.0 - BETA_ONE**STEP) / (jnp.sqrt(two / (1.0 - BETA_TWO**STEP)) + ADAM_EPS)
-        )
-        half = jnp.dot(left[...], direction, precision=HIGHEST, preferred_element_type=F32)
-        turned = lax.dot_general(
-            half,
-            right,
-            (((1,), (1,)), ((), ())),
-            precision=HIGHEST,
-            preferred_element_type=F32,
-        )
-        new = biases[at] - LEARN_RATE * turned
-        copies_out[at] = new.astype(BF16)
-        mine = owners[k] == dp
-        new_out[at] = jnp.where(mine, new, 0.0)
-        one_out[at] = jnp.where(mine, one, 0.0)
-        two_out[at] = jnp.where(mine, two, 0.0)
-
-
-def update_call(*args):
+
+    for fetch, store in zip(fetches, stores):
+        fetch.wait()
+        store.start()
+    half = product(clipped, left[...], 1, 0)
+    rotated = per_matrix(lambda k: product(right_bases[k], half, 0, 0))
+    one = BETA_ONE * moment_one[...] + (1.0 - BETA_ONE) * rotated
+    two = BETA_TWO * moment_two[...] + (1.0 - BETA_TWO) * rotated * rotated
+    direction = (
+        one / (1.0 - BETA_ONE**STEP) / (jnp.sqrt(two / (1.0 - BETA_TWO**STEP)) + ADAM_EPS)
+    )
+    half = per_matrix(lambda k: product(right_bases[k], direction, 1, 0))
+    new = biases[...] - LEARN_RATE * product(half, left[...], 1, 1)
+    copies_out[...] = new.astype(BF16)
+    mine = per_matrix(lambda k: jnp.where(owners[k] == dp, 1.0, 0.0)) > 0.5
+    new_out[...] = jnp.where(mine, new, 0.0)
+    one_out[...] = jnp.where(mine, one, 0.0)
+    two_out[...] = jnp.where(mine, two, 0.0)
+    for store in stores:
+        store.wait()
+
+
+def update_call(tokens, *args):
     in_vmem = pl.BlockSpec(memory_space=pltpu.VMEM)
-    block = jax.ShapeDtypeStruct((BROWS, HD), F32)
+    anywhere = pl.BlockSpec(memory_space=pl.ANY)
+    block = jax.ShapeDtypeStruct((HD, BROWS), F32)
+    wide = jax.ShapeDtypeStruct((tokens, D), BF16)
     return pl.pallas_call(
         update_kernel,
         out_shape=(
             block,
             jax.ShapeDtypeStruct((1, 1), F32),
             block,
-            jax.ShapeDtypeStruct((BROWS, HD), BF16),
+            jax.ShapeDtypeStruct((HD, BROWS), BF16),
             block,
             block,
+            wide,
+            wide,
         ),
-        in_specs=[in_vmem] * 8 + [pl.BlockSpec(memory_space=pltpu.SMEM)],
-        out_specs=(in_vmem,) * 6,
+        in_specs=[in_vmem] * 8 + [pl.BlockSpec(memory_space=pltpu.SMEM)] + [anywhere] * 2,
+        out_specs=(in_vmem,) * 6 + (anywhere,) * 2,
+        scratch_shapes=[
+            pltpu.VMEM((BROWS, HD), F32),
+            pltpu.VMEM((BROWS, BROWS), F32),
+            pltpu.VMEM((2, tokens, D), BF16),
+            pltpu.SemaphoreType.DMA((4,)),
+        ],
         name="update",
     )(*args)
 
@@ -978,34 +1096,39 @@
         output_grad,
         first_gain.reshape(1, D),
         second_gain.reshape(1, D),
-        biases.reshape(1, FLAT),
-        segment_number.reshape(-1, SEQ),
-        token_mask.reshape(-1, SEQ),
+        biases.T,
+        segment_number.reshape(1, -1),
+        token_mask.reshape(1, -1),
         input_project,
         output_project,
         expand_weight,
         reduce_weight,
     )
-    clipped, clip_norm, new_owned, copies, first_owned, second_owned = update_call(
-        sums.reshape(BROWS, HD),
-        biases,
-        first_moment,
-        second_moment,
-        left_pairs,
-        left_hidden,
-        left_small,
-        right_bases,
-        owners,
+    clipped, clip_norm, new_owned, copies, first_owned, second_owned, layer_out, input_grad = (
+        update_call(
+            inputs.shape[0],
+            sums,
+            biases.T,
+            first_moment.T,
+            second_moment.T,
+            left_pairs,
+            left_hidden,
+            left_small,
+            right_bases,
+            owners,
+            layer_out,
+            input_grad,
+        )
     )
     return (
         layer_out,
         input_grad,
-        clipped,
+        clipped.T,
         clip_norm.reshape(1),
-        new_owned,
-        copies,
-        first_owned,
-        second_owned,
+        new_owned.T,
+        copies.T,
+        first_owned.T,
+        second_owned.T,
     )
 
 

time: 162 us -> 117 us (0.72)
  the two profiles are of different devices: /device:TPU:0 before, /device:TPU:12 now
where the time goes in v3:
time: 117 us
  Pallas kernels  114 us (97%)
  local copies, waits for them, and re-layouts  2.59 us (2%)
    pallas_call x1, Pallas kernels, layer_call(): pl.pallas_call(partial(layer_kernel, lay), out_shape=(jax.ShapeDtypeStruc...  109 us
    pallas_call x1, Pallas kernels, update_call(): pl.pallas_call(update_kernel, out_shape=(block, jax.ShapeDtypeStruct((1,...  4.84 us

profile of v3, /device:TPU:12, one launch (start us, length us, event | category | flops | bytes accessed | tf_op | source)
XLA Modules:
  0.0 116.9 jit_solution(17389039236081428323)
XLA Ops:
  0.6 1.3 %reshape.33.seg = s32[1,1536]{1,0:T(1,128)} reshape(s32[1536]{0:T(1024)} %param.33) | data formatting | bytes 12288 | tf_op jit(solution)/shard_map/reshape | solution.py:1100
  1.9 1.3 %reshape.34.val = s32[1,1536]{1,0:T(1,128)} reshape(s32[1536]{0:T(1024)} %param.34) | data formatting | bytes 12288 | tf_op jit(solution)/shard_map/reshape | solution.py:1101
  3.2 108.7 %layer.1 = (bf16[384,1024]{1,0:T(8,128)(2,1)}, bf16[384,1024]{1,0:T(8,128)(2,1)}, f32[1,10240]{1,0:T(1,128)}) custom-call(bf16[384,1024]{1,0:T(8,128)(2,1)} %x.1, bf16[384,1024]{1,0:T(8,128)(2,1)} %og.1, f32[1,1024]{1,0:T(1,128)} %bitcast.15, f32[1,1024]{1,0:T(1,128)} %bitcast.16, f32[64,160]{1,0:T(8,128)} %bitcast.11, s32[1,1536]{1,0:T(1,128)} %reshape.33.seg, ...), custom_call_target="tpu_custom_call" | custom-call | tf_op jit(solution)/shard_map/layer/pallas_call | solution.py:934
  111.9 4.8 %update.1 = (f32[64,160]{1,0:T(8,128)}, f32[1,1]{1,0:T(1,128)}, f32[64,160]{1,0:T(8,128)}, bf16[64,160]{1,0:T(8,128)(2,1)}, f32[64,160]{1,0:T(8,128)}, /*index=5...) custom-call(f32[1,10240]{1,0:T(1,128)} %get-tuple-element.19.raw, f32[64,160]{1,0:T(8,128)} %bitcast.12, ...), custom_call_target="tpu_custom_call" | custom-call | tf_op jit(solution)/shard_map/update/pallas_call | solution.py:1046

commit v4 on v3

--- a/solution.py
+++ b/solution.py
@@ -33,6 +33,7 @@
 F32 = jnp.float32
 
 SUBS = 4
+LAST_SUBS = 4
 RELAY_LAG, LAG = 2, 4
 UNIT = 256
 TILE = 256
@@ -76,8 +77,8 @@
 
 def layer_kernel(
     lay,
-    x,
-    og,
+    x_hbm,
+    og_hbm,
     gain1,
     gain2,
     biases_t,
@@ -91,6 +92,8 @@
     ig_hbm,
     bsum,
     brow,
+    x,
+    og,
     out,
     ig,
     wqkv,
@@ -114,8 +117,6 @@
     hid,
     gp,
     back,
-    dka,
-    dva,
     group_early,
     group_late,
     all_early,
@@ -138,6 +139,8 @@
     sem_ar,
     sem_bs,
     sem_br,
+    sem_up,
+    sem_down,
 ):
     T, S, B, NB, NU = lay.ranks, lay.tokens, lay.block, lay.blocks, lay.units
     W, PP, F = lay.width, lay.pairs, lay.hidden
@@ -195,15 +198,40 @@
 
     barrier = pltpu.get_barrier_semaphore()
     others = [peer(o) for o in range(1, T)]
-    others += [((dp + o) % lay.dp_size, t) for o in range(1, lay.dp_size)]
+    heard = T - 1
+
+    def greet(device):
+        pl.semaphore_signal(barrier, inc=1, device_id=device, device_id_type=MESH_ID)
+
+    if quads:
+        others.append((flip(dp, 1), t))
+        link, links = dp // 2, lay.dp_size // 2
+        before, after = (dp - 2, t), (dp + 2, t)
+
+        @pl.when(link > 0)
+        def _():
+            greet(before)
+
+        @pl.when(link < links - 1)
+        def _():
+            greet(after)
+
+        heard = heard + 1 + jnp.where(link > 0, 1, 0) + jnp.where(link < links - 1, 1, 0)
+    else:
+        others += [((dp + o) % lay.dp_size, t) for o in range(1, lay.dp_size)]
+        heard = len(others)
     for device in others:
-        pl.semaphore_signal(barrier, inc=1, device_id=device, device_id_type=MESH_ID)
+        greet(device)
     local = [
         pltpu.make_async_copy(src, dst, sem_local.at[i])
         for i, (src, dst) in enumerate(zip(sources, pieces(t)))
     ]
+    x_copy = pltpu.make_async_copy(x_hbm, x, sem_out.at[3])
+    x_copy.start()
     for copy in local:
         copy.start()
+    og_copy = pltpu.make_async_copy(og_hbm, og, sem_out.at[2])
+    og_copy.start()
 
     row0 = (NB * t) // NU
     has_b = (NB * t + NB - 1) // NU != row0
@@ -219,23 +247,9 @@
     def block_at(j):
         return pl.ds(j * B, B)
 
-    key_at = lax.broadcasted_iota(jnp.int32, (B, SEQ), 1)
-    query_at = lax.broadcasted_iota(jnp.int32, (B, SEQ), 0)
-    for j in range(NB):
-        u, row, slot, w = place(j)
-        keys_here = pl.ds(pl.multiple_of(row * SEQ, SEQ), SEQ)
-        numbers = seg[:, keys_here].astype(F32)
-        keyed = jnp.where(val[:, keys_here] == 1, numbers, -1.0)
-        same = key_at == query_at + w * B
-        own = jnp.sum(jnp.where(same, numbers, 0.0), axis=1, keepdims=True)
-        mask[j] = jnp.where((own == keyed) | same, 0.0, -1e30)
-        xkv[slot, rows_at(w)] = x[block_at(j)]
-
-    bias_rows = biases_t[...].T
-    for i in range(BROWS):
-        brow[:, i * HD : (i + 1) * HD] = bias_rows[i : i + 1]
-
-    pl.semaphore_wait(barrier, len(others))
+    pl.semaphore_wait(barrier, heard)
+
+    x_copy.wait()
 
     def send_rows():
         for j in range(NB):
@@ -265,21 +279,28 @@
         core, ynext = (dp, rank(1)), (dp, rank(2))
         xnext, znext = (flip(dp, 1), t), (flip(dp, 2), t)
         rounds = 4
-        steps = rounds * SUBS
-        part_a, part_b = D // SUBS, UNIT // SUBS
+        tail_step = (rounds - 1) * SUBS
+        steps = tail_step + LAST_SUBS
+        part_a, part_b, part_c = D // SUBS, UNIT // SUBS, UNIT // LAST_SUBS
 
         def chunk(idx, g, fn):
-            n = (idx // SUBS * 3 + g) * SUBS + idx % SUBS
+            n = g * steps + idx
 
             @pl.when((idx >= 0) & (idx < SUBS))
             def _():
                 at = pl.ds(pl.multiple_of(idx * part_a, part_a), part_a)
                 fn(lambda r: wqkv.at[r, g, at], n)
 
-            @pl.when((idx >= SUBS) & (idx < steps))
+            @pl.when((idx >= SUBS) & (idx < tail_step))
             def _():
                 row = ((idx // SUBS - 1) * 3 + g) * UNIT + (idx % SUBS) * part_b
                 at = pl.ds(pl.multiple_of(row, part_b), part_b)
+                fn(lambda r: big.at[r, at], n)
+
+            @pl.when((idx >= tail_step) & (idx < steps))
+            def _():
+                row = ((rounds - 2) * 3 + g) * UNIT + (idx - tail_step) * part_c
+                at = pl.ds(pl.multiple_of(row, part_c), part_c)
                 fn(lambda r: big.at[r, at], n)
 
         def send_y(idx):
@@ -343,27 +364,27 @@
                 remote(view(t), view(t), sem_x.at[idx], sem_w.at[n], xnext).wait_send()
                 remote(view(t), view(t), sem_z.at[idx], sem_w.at[n], znext).wait_send()
                 for g in range(3):
-                    m = (idx // SUBS * 3 + g) * SUBS + idx % SUBS
+                    m = g * steps + idx
                     remote(view(t), view(t), sem_c.at[m], sem_p.at[m], core).wait_send()
 
             chunk(idx, gy, go)
             return carry
 
         def from_partner(unit_low, unit_high):
-            def go(n, carry):
-                @pl.when(n < 3 * SUBS)
-                def _():
+            for unit in range(unit_low, unit_high):
+                p, g = unit // 3, unit % 3
+                low_step = p * SUBS
+                if p == 0:
                     view = wqkv.at[rank(3), 0, pl.ds(0, part_a)]
+                else:
+                    view = big.at[rank(3), pl.ds(0, part_c if p == rounds - 1 else part_b)]
+
+                def go(idx, carry):
+                    n = g * steps + idx
                     remote(view, view, sem_c.at[n], sem_p.at[n], core).wait_recv()
-
-                @pl.when(n >= 3 * SUBS)
-                def _():
-                    view = big.at[rank(3), pl.ds(0, part_b)]
-                    remote(view, view, sem_c.at[n], sem_p.at[n], core).wait_recv()
-
-                return carry
-
-            lax.fori_loop(unit_low * SUBS, unit_high * SUBS, go, 0)
+                    return carry
+
+                lax.fori_loop(low_step, steps if p == rounds - 1 else low_step + SUBS, go, 0)
 
         def own_copies(i):
             return remote(sources[i], pieces(t)[i], sem_own_s.at[i], sem_own_r.at[i], core)
@@ -412,6 +433,22 @@
                 remote(
                     sources[i], pieces(rank(o))[i], sem_own_s.at[n], sem_own_r.at[n], peer(o)
                 ).wait_recv()
+
+    key_at = lax.broadcasted_iota(jnp.int32, (B, SEQ), 1)
+    query_at = lax.broadcasted_iota(jnp.int32, (B, SEQ), 0)
+    for j in range(NB):
+        u, row, slot, w = place(j)
+        keys_here = pl.ds(pl.multiple_of(row * SEQ, SEQ), SEQ)
+        numbers = seg[keys_here].reshape(1, SEQ).astype(F32)
+        keyed = jnp.where(val[keys_here].reshape(1, SEQ) == 1, numbers, -1.0)
+        same = key_at == query_at + w * B
+        own = jnp.sum(jnp.where(same, numbers, 0.0), axis=1, keepdims=True)
+        mask[j] = jnp.where((own == keyed) | same, 0.0, -1e30)
+        xkv[slot, rows_at(w)] = x[block_at(j)]
+
+    bias_rows = biases_t[...].T
+    for i in range(BROWS):
+        brow[:, i * HD : (i + 1) * HD] = bias_rows[i : i + 1]
 
     head_lane = lax.broadcasted_iota(jnp.int32, (B, PAIR), 1) < HD
 
@@ -475,7 +512,7 @@
             scores = nt(query, kbuf[hp, slot]) + jnp.concatenate([hide, hide], axis=0)
             peak = jnp.max(scores, axis=1, keepdims=True)
             probs = jnp.exp(scores - peak).astype(BF16)
-            pbuf[hp, j] = probs
+            pbuf[hp, j * 2 * B : (j + 1) * 2 * B] = probs
             mixed = nn(probs, jnp.concatenate([vbuf[hp, slot], ones], axis=1))
             inverse = 1.0 / join_heads(mixed[:, PAIR:])
             linv[hp, block_at(j)] = inverse
@@ -543,8 +580,7 @@
             bbuf[:, at] = bbuf[:, at] + nn(hid[r], w2(r)[:, n : n + TILE])
 
     if quads:
-        whole = [(k + 1) * SUBS + LAG - 1 for k in range(rounds)]
-        mid = SUBS // 2
+        whole = [(k + 1) * SUBS + LAG - 1 for k in range(rounds - 1)] + [steps + LAG - 1]
         plan = [
             (project, [PLAN[0], PLAN[1], whole[0], whole[0] + 2]),
             (attend_rank, [PLAN[2], PLAN[3], whole[0] + 1, whole[0] + 3]),
@@ -552,8 +588,21 @@
             (reduce, [whole[1] + 3, whole[1] + 4, whole[3], whole[3]]),
         ]
 
+        def pass_on(place_in_chain, sem, to, s):
+            @pl.when(s == 2 * place_in_chain)
+            def _():
+                @pl.when(place_in_chain > 0)
+                def _():
+                    pl.semaphore_wait(sem, 1)
+
+                @pl.when(place_in_chain < links - 1)
+                def _():
+                    pl.semaphore_signal(sem, inc=1, device_id=to, device_id_type=MESH_ID)
+
         def step(s, carry):
             service(s, 0)
+            pass_on(link, sem_up, after, s)
+            pass_on(links - 1 - link, sem_down, before, s)
 
             @pl.when(s == whole[1])
             def _():
@@ -585,6 +634,7 @@
         each_rank(reduce)
 
     nought_row = jnp.zeros((1, D), F32)
+    og_copy.wait()
 
     def norm_second(at, carry):
         sum_up, sum_second = carry
@@ -692,46 +742,53 @@
 
     in_group = [peer(o) for o in range(1, T)]
     in_dp = [((dp + o) % lay.dp_size, t) for o in range(1, lay.dp_size)]
-    early = Totals(0, AT_HIDDEN, FLAT - AT_HIDDEN, group_early, all_early)
-    late = Totals(1, AT_QUERY, AT_HIDDEN, group_late, all_late)
+    early = Totals(0, AT_VALUE, FLAT - AT_VALUE, group_early, all_early)
+    late = Totals(1, AT_QUERY, AT_VALUE, group_late, all_late)
+
+    for r in range(T):
+        grad = nt(low[...], wo(r)[...]).astype(BF16)
+        cgrad[r] = grad
+        bsum[:, AT_VALUE + r * W : AT_VALUE + (r + 1) * W] = jnp.sum(
+            grad.astype(F32), axis=0, keepdims=True
+        )
     early.start()
 
-    for r in range(T):
-        cgrad[r] = nt(low[...], wo(r)[...]).astype(BF16)
-
-    def attend_back(r, i):
+    lone = jnp.where(place(1)[1] != place(0)[1], 0, NB - 1)
+    pair_at = jnp.where(lone == 0, 1, 0)
+    slot_pair = (NB * t + pair_at) // NU - row0
+    slot_lone = (NB * t + lone) // NU - row0
+    slot_kept = jnp.where(has_b, slot_pair, 1)
+
+    def attend_back(r, i, first_block, amount, slot):
         hp = r * PP + i
-        dka[...] = jnp.zeros_like(dka)
-        dva[...] = jnp.zeros_like(dva)
-        query_sum = jnp.zeros((1, PAIR), F32)
-        for j in range(NB):
-            u, row, slot, w = place(j)
-            lanes = pl.ds(i * PAIR, PAIR)
-            scaled = cgrad[r, block_at(j), lanes].astype(F32) * linv[hp, block_at(j)]
-            upstream = split_heads(scaled.astype(BF16))
-            delta = jnp.sum(
-                split_heads(scaled * ctx[r, block_at(j), lanes].astype(F32)), axis=1, keepdims=True
-            )
-            probs = pbuf[hp, j]
-            query = split_heads(qbuf[hp, block_at(j)])
-            score = (probs.astype(F32) * (nt(upstream, vbuf[hp, slot]) - delta)).astype(BF16)
-            dva[slot] += tn(probs, upstream)
-            dka[slot] += tn(score, query)
-            grad = join_heads(nn(score, kbuf[hp, slot])) * HD**-0.5
-            qbuf[hp, block_at(j)] = grad.astype(BF16)
-            query_sum = query_sum + jnp.sum(grad, axis=0, keepdims=True)
-        value_sum = jnp.zeros((1, PAIR), F32)
-        for slot in range(2):
-            kbuf[hp, slot] = dka[slot].astype(BF16)
-            vbuf[hp, slot] = dva[slot].astype(BF16)
-            value_sum = value_sum + jnp.sum(dva[slot], axis=0, keepdims=True)
-        lanes = pl.multiple_of(r * W + i * PAIR, PAIR)
-        bsum[:, pl.ds(AT_QUERY + lanes, PAIR)] = query_sum
-        bsum[:, pl.ds(AT_VALUE + lanes, PAIR)] = value_sum
-
-    def rank_back(r, carry):
+        lanes = pl.ds(i * PAIR, PAIR)
+        queries, upstreams, deltas = [], [], []
+        for k in range(amount):
+            at = rows_at(first_block + k)
+            scaled = cgrad[r, at, lanes].astype(F32) * linv[hp, at]
+            upstreams.append(split_heads(scaled.astype(BF16)))
+            deltas.append(split_heads(scaled * ctx[r, at, lanes].astype(F32)))
+            queries.append(split_heads(qbuf[hp, at]))
+        upstream, query = jnp.concatenate(upstreams), jnp.concatenate(queries)
+        delta = jnp.sum(jnp.concatenate(deltas), axis=1, keepdims=True)
+        probs = pbuf[hp, pl.ds(pl.multiple_of(first_block * 2 * B, 2 * B), amount * 2 * B)]
+        score = (probs.astype(F32) * (nt(upstream, vbuf[hp, slot]) - delta)).astype(BF16)
+        value_grad = nn(upstream.T, probs)
+        key_grad = nn(query.T, score)
+        joined = nn(score, kbuf[hp, slot]) * HD**-0.5
+        total = jnp.zeros((1, PAIR), F32)
+        for k in range(amount):
+            grad = join_heads(joined[k * 2 * B : (k + 1) * 2 * B])
+            qbuf[hp, rows_at(first_block + k)] = grad.astype(BF16)
+            total = total + jnp.sum(grad, axis=0, keepdims=True)
+        return key_grad.astype(BF16).T, value_grad.astype(BF16).T, total
+
+    def rank_back_pair(r, carry):
         for i in range(PP):
-            attend_back(r, i)
+            keys, values, total = attend_back(r, i, pair_at, 2, slot_pair)
+            kbuf[r * PP + i, slot_kept] = keys
+            vbuf[r * PP + i, slot_kept] = values
+            bsum[:, pl.ds(pl.multiple_of(AT_QUERY + r * W + i * PAIR, PAIR), PAIR)] = total
 
         @pl.when(r == T // 2 - 1)
         def _():
@@ -739,57 +796,80 @@
 
         return carry
 
-    lax.fori_loop(0, T, rank_back, 0)
-    late.start()
+    def rank_back_lone(r, carry):
+        for i in range(PP):
+            hp = r * PP + i
+            keys, values, total = attend_back(r, i, lone, 1, slot_lone)
+            at = pl.ds(pl.multiple_of(AT_QUERY + r * W + i * PAIR, PAIR), PAIR)
+            bsum[:, at] = bsum[:, at] + total
+            kept = [jnp.where(has_b, jnp.zeros_like(keys), buf[hp, 1]) for buf in (kbuf, vbuf)]
+            kbuf[hp, slot_lone] = keys + kept[0]
+            vbuf[hp, slot_lone] = values + kept[1]
+        return carry
 
     def wide(buffer, r, *at):
         return jnp.concatenate([buffer[(r * PP + i, *at)] for i in range(PP)], axis=1)
 
-    def shares(slot):
-        def body(k, carry):
-            at = pl.ds(pl.multiple_of(k * TILE, TILE), TILE)
-            total = nt(wide(kbuf, 0, slot), wqkv[0, 1, at])
-            total = total + nt(wide(vbuf, 0, slot), wqkv[0, 2, at])
-            for r in range(1, T):
-                total = total + nt(wide(kbuf, r, slot), wqkv[r, 1, at])
-                total = total + nt(wide(vbuf, r, slot), wqkv[r, 2, at])
-            xkv[slot, :, at] = total.astype(BF16)
-            return carry
-
-        lax.fori_loop(0, D // TILE, body, 0)
-
-    def share_copy(slot, w):
+    half = SEQ // 2
+
+    def share_copy(slot, w, k):
         u = (row0 + slot) * NU + w
         owner = u // NB
         first = (row0 + slot) * NU // NB
         place_of = t - first - jnp.where(t > owner, 1, 0)
         number = (u - owner * NB) * (lay.span - 1) + place_of
+        at = pl.ds(pl.multiple_of(k * TILE, TILE), TILE)
         return remote(
-            xkv.at[slot, rows_at(w)],
-            back.at[number],
-            sem_gs.at[slot * NU + w],
-            sem_gr.at[number],
+            xkv.at[slot, rows_at(w), at],
+            back.at[number, :, at],
+            sem_gs.at[slot * NU + w, k],
+            sem_gr.at[number, k],
             (dp, owner),
         )
 
-    def send_shares(turn, carry):
-        slot = (1 - slot_first + turn) % 2
-
-        @pl.when((slot == 0) | has_b)
-        def _():
-            shares(slot)
-            for w in range(NU):
+    def send_shares(slot, rows, first_unit, amount):
+        def body(k, carry):
+            at = pl.ds(pl.multiple_of(k * TILE, TILE), TILE)
+            total = nt(wide(kbuf, 0, slot, rows), wqkv[0, 1, at])
+            total = total + nt(wide(vbuf, 0, slot, rows), wqkv[0, 2, at])
+            for r in range(1, T):
+                total = total + nt(wide(kbuf, r, slot, rows), wqkv[r, 1, at])
+                total = total + nt(wide(vbuf, r, slot, rows), wqkv[r, 2, at])
+            xkv[slot, rows, at] = total.astype(BF16)
+            for n in range(amount):
+                w = first_unit + n
                 owner = ((row0 + slot) * NU + w) // NB
 
                 @pl.when(owner != t)
                 def _():
-                    share_copy(slot, w).start()
+                    share_copy(slot, w, k).start()
+
+            return carry
+
+        lax.fori_loop(0, D // TILE, body, 0)
+
+    def send_half(slot, part):
+        rows = pl.ds(pl.multiple_of(part * half, half), half)
+        send_shares(slot, rows, part * (NU // 2), NU // 2)
+
+    lax.fori_loop(0, T, rank_back_pair, 0)
+    part_first = jnp.where(lone == 0, 1, 0)
+
+    def turns(k, carry):
+        @pl.when((k != 1) & has_b)
+        def _():
+            send_half(slot_pair, jnp.where(k == 0, part_first, 1 - part_first))
+
+        @pl.when(k == 1)
+        def _():
+            lax.fori_loop(0, T, rank_back_lone, 0)
+            late.start()
 
         return carry
 
-    lax.fori_loop(0, 2, send_shares, 0)
+    lax.fori_loop(0, 3, turns, 0)
     late.middle()
-    early.finish()
+    send_shares(slot_lone, pl.ds(0, SEQ), 0, NU)
 
     for n in range(0, D, TILE):
         total = nt(wide(qbuf, 0), wqkv[0, 0, pl.ds(n, TILE)])
@@ -800,22 +880,28 @@
 
     for j in range(NB):
         u, row, slot, w = place(j)
+        bbuf[block_at(j)] = bbuf[block_at(j)] + xkv[slot, rows_at(w)].astype(F32)
+    early.finish()
+
+    for j in range(NB):
+        u, row, slot, w = place(j)
         first = row * NU // NB
         last = (row * NU + NU - 1) // NB
-        bbuf[block_at(j)] = bbuf[block_at(j)] + xkv[slot, rows_at(w)].astype(F32)
         for o in range(lay.span - 1):
             number = j * (lay.span - 1) + o
 
             @pl.when(first + o < last)
             def _():
                 sender = first + o + jnp.where(first + o >= t, 1, 0)
-                remote(
-                    xkv.at[0, rows_at(0)],
-                    back.at[number],
-                    sem_gs.at[0],
-                    sem_gr.at[number],
-                    (dp, sender),
-                ).wait_recv()
+                for k in range(D // TILE):
+                    at = pl.ds(k * TILE, TILE)
+                    remote(
+                        xkv.at[0, rows_at(0), at],
+                        back.at[number, :, at],
+                        sem_gs.at[0, k],
+                        sem_gr.at[number, k],
+                        (dp, sender),
+                    ).wait_recv()
                 bbuf[block_at(j)] = bbuf[block_at(j)] + back[number].astype(F32)
 
         ig[block_at(j)] = bbuf[block_at(j)].astype(BF16)
@@ -832,7 +918,7 @@
 
             @pl.when((owner != t) & ((slot == 0) | has_b))
             def _():
-                share_copy(slot, w).wait_send()
+                lax.fori_loop(0, D // TILE, lambda k, c: (share_copy(slot, w, k).wait_send(), c)[1], 0)
 
     for j in range(NB):
         u, row, slot, w = place(j)
@@ -878,11 +964,11 @@
             vmem((T, lay.hidden, D), BF16),
         ]
     dma = pltpu.SemaphoreType.DMA
-    steps = 4 * SUBS
+    steps = 3 * SUBS + LAST_SUBS
     own = 4 if lay.quads else 4 * T
     sharers = lay.blocks * max(lay.span - 1, 1)
     scratch = (
-        [vmem((1, FLAT), F32), vmem((S, D), BF16), vmem((S, D), BF16)]
+        [vmem((1, FLAT), F32)] + [vmem((S, D), BF16)] * 4
         + [vmem((T, 3, D, lay.width), BF16)]
         + wide
         + [
@@ -890,7 +976,7 @@
             vmem((hp, S, PAIR), BF16),
             vmem((hp, 2, SEQ, PAIR), BF16),
             vmem((hp, 2, SEQ, PAIR), BF16),
-            vmem((hp, lay.blocks, 2 * lay.block, SEQ), BF16),
+            vmem((hp, lay.blocks * 2 * lay.block, SEQ), BF16),
             vmem((hp, S, PAIR), F32),
             vmem((lay.blocks, lay.block, SEQ), F32),
             vmem((T, S, lay.width), BF16),
@@ -903,14 +989,12 @@
             vmem((T, S, lay.hidden), BF16),
             vmem((T, S, lay.hidden), BF16),
             vmem((sharers, lay.block, D), BF16),
-            vmem((2, SEQ, PAIR), F32),
-            vmem((2, SEQ, PAIR), F32),
-            vmem((T, 1, FLAT - AT_HIDDEN), F32),
-            vmem((T, 1, AT_HIDDEN), F32),
-            vmem((lay.dp_size, 1, FLAT - AT_HIDDEN), F32),
-            vmem((lay.dp_size, 1, AT_HIDDEN), F32),
+            vmem((T, 1, FLAT - AT_VALUE), F32),
+            vmem((T, 1, AT_VALUE), F32),
+            vmem((lay.dp_size, 1, FLAT - AT_VALUE), F32),
+            vmem((lay.dp_size, 1, AT_VALUE), F32),
             dma((4,)),
-            dma((2,)),
+            dma((4,)),
             dma((own,)),
             dma((own,)),
             dma((steps,)),
@@ -921,12 +1005,14 @@
             dma((3 * steps,)),
             dma((lay.blocks * lay.span,)),
             dma((2 * lay.units,)),
-            dma((2 * lay.units,)),
-            dma((sharers,)),
+            dma((2 * lay.units, D // TILE)),
+            dma((sharers, D // TILE)),
             dma((2, T)),
             dma((2, T)),
             dma((2, lay.dp_size)),
             dma((2, lay.dp_size)),
+            pltpu.SemaphoreType.REGULAR,
+            pltpu.SemaphoreType.REGULAR,
         ]
     )
     in_vmem = pl.BlockSpec(memory_space=pltpu.VMEM)
@@ -938,7 +1024,7 @@
             jax.ShapeDtypeStruct((S, D), BF16),
             jax.ShapeDtypeStruct((1, FLAT), F32),
         ),
-        in_specs=[in_vmem] * 7 + [anywhere] * 4,
+        in_specs=[anywhere] * 2 + [in_vmem] * 5 + [anywhere] * 4,
         out_specs=(anywhere, anywhere, in_vmem),
         scratch_shapes=scratch,
         compiler_params=pltpu.CompilerParams(
@@ -1000,6 +1086,9 @@
     left[...] = jnp.zeros_like(left)
     for begin, amount, basis in layout:
         left[begin : begin + amount, begin : begin + amount] = basis[...]
+    for fetch, store in zip(fetches, stores):
+        fetch.wait()
+        store.start()
     column = lax.broadcasted_iota(jnp.int32, (HD, BROWS), 1)
 
     def per_matrix(choose):
@@ -1017,9 +1106,6 @@
             preferred_element_type=F32,
         )
 
-    for fetch, store in zip(fetches, stores):
-        fetch.wait()
-        store.start()
     half = product(clipped, left[...], 1, 0)
     rotated = per_matrix(lambda k: product(right_bases[k], half, 0, 0))
     one = BETA_ONE * moment_one[...] + (1.0 - BETA_ONE) * rotated
@@ -1097,8 +1183,8 @@
         first_gain.reshape(1, D),
         second_gain.reshape(1, D),
         biases.T,
-        segment_number.reshape(1, -1),
-        token_mask.reshape(1, -1),
+        segment_number,
+        token_mask,
         input_project,
         output_project,
         expand_weight,

time: 117 us -> 113 us (0.966)
  the two profiles are of different devices: /device:TPU:12 before, /device:TPU:0 now
where the time goes in v4:
time: 113 us; the launch traced here: 112 us
  Pallas kernels  112 us (99%)
    pallas_call x1, Pallas kernels, layer_call(): pl.pallas_call(partial(layer_kernel, lay), out_shape=(jax.ShapeDtypeStruc...  107 us
    pallas_call x1, Pallas kernels, update_call(): pl.pallas_call(update_kernel, out_shape=(block, jax.ShapeDtypeStruct((1,...  4.84 us

profile of v4, /device:TPU:0, one launch (start us, length us, event | category | flops | bytes accessed | tf_op | source)
XLA Modules:
  0.0 112.5 jit_solution(14508799726682506407)
XLA Ops:
  0.6 106.8 %layer.1 = (bf16[384,1024]{1,0:T(8,128)(2,1)}, bf16[384,1024]{1,0:T(8,128)(2,1)}, f32[1,10240]{1,0:T(1,128)}) custom-call(bf16[384,1024]{1,0:T(8,128)(2,1)} %x_hbm.1, bf16[384,1024]{1,0:T(8,128)(2,1)} %og_hbm.1, f32[1,1024]{1,0:T(1,128)} %bitcast.15, f32[1,1024]{1,0:T(1,128)} %bitcast.16, f32[64,160]{1,0:T(8,128)} %bitcast.11, s32[1536]{0:T(1024)} %seg.1, ...), custom_call_target="tpu_custom_call" | custom-call | tf_op jit(solution)/shard_map/layer/pallas_call | solution.py:1020
  107.5 4.8 %update.1 = (f32[64,160]{1,0:T(8,128)}, f32[1,1]{1,0:T(1,128)}, f32[64,160]{1,0:T(8,128)}, bf16[64,160]{1,0:T(8,128)(2,1)}, f32[64,160]{1,0:T(8,128)}, /*index=5...) custom-call(f32[1,10240]{1,0:T(1,128)} %get-tuple-element.19.raw, f32[64,160]{1,0:T(8,128)} %bitcast.12, ...), custom_call_target="tpu_custom_call" | custom-call | tf_op jit(solution)/shard_map/update/pallas_call | solution.py:1132

commit v5 on v4

--- a/solution.py
+++ b/solution.py
@@ -34,6 +34,7 @@
 
 SUBS = 4
 LAST_SUBS = 4
+DIRECT = 2
 RELAY_LAG, LAG = 2, 4
 UNIT = 256
 TILE = 256
@@ -79,11 +80,11 @@
     lay,
     x_hbm,
     og_hbm,
-    gain1,
-    gain2,
-    biases_t,
-    seg,
-    val,
+    gain1_hbm,
+    gain2_hbm,
+    biases_hbm,
+    seg_hbm,
+    val_hbm,
     wqkv_in,
     wo_in,
     w1_in,
@@ -96,6 +97,11 @@
     og,
     out,
     ig,
+    gain1,
+    gain2,
+    biases_t,
+    seg,
+    val,
     wqkv,
     wo_b,
     w1_b,
@@ -232,6 +238,20 @@
         copy.start()
     og_copy = pltpu.make_async_copy(og_hbm, og, sem_out.at[2])
     og_copy.start()
+    small = [
+        pltpu.make_async_copy(src, dst, sem_out.at[4 + i])
+        for i, (src, dst) in enumerate(
+            [
+                (biases_hbm, biases_t),
+                (seg_hbm, seg),
+                (val_hbm, val),
+                (gain1_hbm, gain1),
+                (gain2_hbm, gain2),
+            ]
+        )
+    ]
+    for copy in small:
+        copy.start()
 
     row0 = (NB * t) // NU
     has_b = (NB * t + NB - 1) // NU != row0
@@ -303,11 +323,24 @@
                 at = pl.ds(pl.multiple_of(row, part_c), part_c)
                 fn(lambda r: big.at[r, at], n)
 
+        relayed = steps - DIRECT
+        g_direct = jnp.where(role == 1, 2, 1)
+        is_served = (role == 1) | (role == 2)
+
         def send_y(idx):
             def go(view, n):
                 remote(view(t), view(t), sem_y.at[idx], sem_w.at[n], ynext).start()
 
             chunk(idx, gy, go)
+
+            def go_direct(view, n):
+                remote(
+                    view(t), view(t), sem_y.at[idx + DIRECT], sem_w.at[n], ynext
+                ).start()
+
+            @pl.when((idx >= relayed) & is_served)
+            def _():
+                chunk(idx, g_direct, go_direct)
 
         def to_core(view, n):
             remote(view(far), view(far), sem_c.at[n], sem_p.at[n], core).start()
@@ -339,7 +372,7 @@
             def from_x(view, n):
                 arrived(view, n)
 
-                @pl.when(relay)
+                @pl.when(relay & (late < relayed))
                 def _():
                     to_z(view, n, late)
 
@@ -348,7 +381,7 @@
             def from_z(view, n):
                 arrived(view, n)
 
-                @pl.when(relay)
+                @pl.when(relay & (late < relayed))
                 def _():
                     to_x(view, n, late)
 
@@ -361,8 +394,18 @@
         def sent(idx, carry):
             def go(view, n):
                 remote(view(t), view(t), sem_y.at[idx], sem_w.at[n], ynext).wait_send()
-                remote(view(t), view(t), sem_x.at[idx], sem_w.at[n], xnext).wait_send()
-                remote(view(t), view(t), sem_z.at[idx], sem_w.at[n], znext).wait_send()
+
+                @pl.when((role != 3) | (idx < relayed))
+                def _():
+                    remote(view(t), view(t), sem_x.at[idx], sem_w.at[n], xnext).wait_send()
+                    remote(view(t), view(t), sem_z.at[idx], sem_w.at[n], znext).wait_send()
+
+                @pl.when((idx >= relayed) & is_served)
+                def _():
+                    remote(
+                        view(t), view(t), sem_y.at[idx + DIRECT], sem_w.at[n], ynext
+                    ).wait_send()
+
                 for g in range(3):
                     m = g * steps + idx
                     remote(view(t), view(t), sem_c.at[m], sem_p.at[m], core).wait_send()
@@ -370,10 +413,9 @@
             chunk(idx, gy, go)
             return carry
 
-        def from_partner(unit_low, unit_high):
-            for unit in range(unit_low, unit_high):
+        def from_partner(units):
+            for unit in units:
                 p, g = unit // 3, unit % 3
-                low_step = p * SUBS
                 if p == 0:
                     view = wqkv.at[rank(3), 0, pl.ds(0, part_a)]
                 else:
@@ -384,7 +426,10 @@
                     remote(view, view, sem_c.at[n], sem_p.at[n], core).wait_recv()
                     return carry
 
-                lax.fori_loop(low_step, steps if p == rounds - 1 else low_step + SUBS, go, 0)
+                if p == rounds - 1:
+                    lax.fori_loop(tail_step, steps, go, 0)
+                else:
+                    lax.fori_loop(p * SUBS, (p + 1) * SUBS, go, 0)
 
         def own_copies(i):
             return remote(sources[i], pieces(t)[i], sem_own_s.at[i], sem_own_r.at[i], core)
@@ -409,7 +454,7 @@
 
             @pl.when(o == 3)
             def _():
-                from_partner(first_unit[i], first_unit[i + 1])
+                from_partner(range(first_unit[i], first_unit[i + 1]))
 
     else:
 
@@ -434,6 +479,8 @@
                     sources[i], pieces(rank(o))[i], sem_own_s.at[n], sem_own_r.at[n], peer(o)
                 ).wait_recv()
 
+    for copy in small:
+        copy.wait()
     key_at = lax.broadcasted_iota(jnp.int32, (B, SEQ), 1)
     query_at = lax.broadcasted_iota(jnp.int32, (B, SEQ), 0)
     for j in range(NB):
@@ -585,7 +632,7 @@
             (project, [PLAN[0], PLAN[1], whole[0], whole[0] + 2]),
             (attend_rank, [PLAN[2], PLAN[3], whole[0] + 1, whole[0] + 3]),
             (expand, [whole[1] + 1, whole[1] + 2, whole[2], whole[2] + 1]),
-            (reduce, [whole[1] + 3, whole[1] + 4, whole[3], whole[3]]),
+            (reduce, [whole[1] + 3, whole[1] + 4]),
         ]
 
         def pass_on(place_in_chain, sem, to, s):
@@ -855,19 +902,17 @@
     lax.fori_loop(0, T, rank_back_pair, 0)
     part_first = jnp.where(lone == 0, 1, 0)
 
-    def turns(k, carry):
-        @pl.when((k != 1) & has_b)
+    lax.fori_loop(0, T, rank_back_lone, 0)
+    late.start()
+
+    def halves(k, carry):
+        @pl.when(has_b)
         def _():
-            send_half(slot_pair, jnp.where(k == 0, part_first, 1 - part_first))
-
-        @pl.when(k == 1)
-        def _():
-            lax.fori_loop(0, T, rank_back_lone, 0)
-            late.start()
+            send_half(slot_pair, (part_first + k) % 2)
 
         return carry
 
-    lax.fori_loop(0, 3, turns, 0)
+    lax.fori_loop(0, 2, halves, 0)
     late.middle()
     send_shares(slot_lone, pl.ds(0, SEQ), 0, NU)
 
@@ -882,6 +927,32 @@
         u, row, slot, w = place(j)
         bbuf[block_at(j)] = bbuf[block_at(j)] + xkv[slot, rows_at(w)].astype(F32)
     early.finish()
+
+    for j in range(NB):
+        u, row, slot, w = place(j)
+        first = row * NU // NB
+        last = (row * NU + NU - 1) // NB
+        for o in range(lay.span):
+            dest = first + o
+
+            @pl.when((dest <= last) & (dest != t))
+            def _():
+                remote(
+                    x.at[block_at(j)],
+                    xkv.at[0, rows_at(0)],
+                    sem_hs.at[j * lay.span + o],
+                    sem_hr.at[0],
+                    (dp, dest),
+                ).wait_send()
+
+    if quads:
+        for i in range(4):
+            own_copies(i).wait_send()
+        lax.fori_loop(0, steps, sent, 0)
+    else:
+        for i in range(4):
+            for o in range(1, T):
+                own_copies(i, o).wait_send()
 
     for j in range(NB):
         u, row, slot, w = place(j)
@@ -919,32 +990,6 @@
             @pl.when((owner != t) & ((slot == 0) | has_b))
             def _():
                 lax.fori_loop(0, D // TILE, lambda k, c: (share_copy(slot, w, k).wait_send(), c)[1], 0)
-
-    for j in range(NB):
-        u, row, slot, w = place(j)
-        first = row * NU // NB
-        last = (row * NU + NU - 1) // NB
-        for o in range(lay.span):
-            dest = first + o
-
-            @pl.when((dest <= last) & (dest != t))
-            def _():
-                remote(
-                    x.at[block_at(j)],
-                    xkv.at[0, rows_at(0)],
-                    sem_hs.at[j * lay.span + o],
-                    sem_hr.at[0],
-                    (dp, dest),
-                ).wait_send()
-
-    if quads:
-        for i in range(4):
-            own_copies(i).wait_send()
-        lax.fori_loop(0, steps, sent, 0)
-    else:
-        for i in range(4):
-            for o in range(1, T):
-                own_copies(i, o).wait_send()
 
 
 def layer_call(lay, *args):
@@ -968,7 +1013,11 @@
     own = 4 if lay.quads else 4 * T
     sharers = lay.blocks * max(lay.span - 1, 1)
     scratch = (
-        [vmem((1, FLAT), F32)] + [vmem((S, D), BF16)] * 4
+        [vmem((1, FLAT), F32)]
+        + [vmem((S, D), BF16)] * 4
+        + [vmem((1, D), F32)] * 2
+        + [vmem((HD, BROWS), F32)]
+        + [vmem((T * S,), jnp.int32)] * 2
         + [vmem((T, 3, D, lay.width), BF16)]
         + wide
         + [
@@ -994,10 +1043,10 @@
             vmem((lay.dp_size, 1, FLAT - AT_VALUE), F32),
             vmem((lay.dp_size, 1, AT_VALUE), F32),
             dma((4,)),
-            dma((4,)),
+            dma((9,)),
             dma((own,)),
             dma((own,)),
-            dma((steps,)),
+            dma((steps + DIRECT,)),
             dma((steps,)),
             dma((steps,)),
             dma((3 * steps,)),
@@ -1024,7 +1073,7 @@
             jax.ShapeDtypeStruct((S, D), BF16),
             jax.ShapeDtypeStruct((1, FLAT), F32),
         ),
-        in_specs=[anywhere] * 2 + [in_vmem] * 5 + [anywhere] * 4,
+        in_specs=[anywhere] * 11,
         out_specs=(anywhere, anywhere, in_vmem),
         scratch_shapes=scratch,
         compiler_params=pltpu.CompilerParams(
@@ -1036,6 +1085,7 @@
 
 VMEM_BYTES = 63 * 2**20
 PLAN = [2, 5, 3, 6]
+PARTS = 4
 
 
 def update_kernel(
@@ -1063,12 +1113,17 @@
     wide,
     sems,
 ):
+    amount = out_in.shape[0] // PARTS
+    parts = [pl.ds(k * amount, amount) for k in range(PARTS)]
     fetches = [
-        pltpu.make_async_copy(src, wide.at[i], sems.at[i]) for i, src in enumerate((out_in, ig_in))
+        pltpu.make_async_copy(src.at[at], wide.at[i, at], sems.at[0, i, k])
+        for i, src in enumerate((out_in, ig_in))
+        for k, at in enumerate(parts)
     ]
     stores = [
-        pltpu.make_async_copy(wide.at[i], dst, sems.at[2 + i])
+        pltpu.make_async_copy(wide.at[i, at], dst.at[at], sems.at[1, i, k])
         for i, dst in enumerate((out_out, ig_out))
+        for k, at in enumerate(parts)
     ]
     for fetch in fetches:
         fetch.start()
@@ -1147,7 +1202,7 @@
             pltpu.VMEM((BROWS, HD), F32),
             pltpu.VMEM((BROWS, BROWS), F32),
             pltpu.VMEM((2, tokens, D), BF16),
-            pltpu.SemaphoreType.DMA((4,)),
+            pltpu.SemaphoreType.DMA((2, 2, PARTS)),
         ],
         name="update",
     )(*args)

time: 113 us -> 106 us (0.938)
  Pallas kernels: 112 us -> 105 us
    pallas_call x1, Pallas kernels: 107 us -> 99.5 us  [layer_call(): pl.pallas_call(partial(layer_kernel, lay), out_shape=(jax.ShapeDtypeStruc...]
where the time goes in v5:
time: 106 us; the launch traced here: 105 us
  Pallas kernels  105 us (99%)
    pallas_call x1, Pallas kernels, layer_call(): pl.pallas_call(partial(layer_kernel, lay), out_shape=(jax.ShapeDtypeStruc...  99.5 us
    pallas_call x1, Pallas kernels, update_call(): pl.pallas_call(update_kernel, out_shape=(block, jax.ShapeDtypeStruct((1,...  5.06 us

profile of v5, /device:TPU:0, one launch (start us, length us, event | category | flops | bytes accessed | tf_op | source)
XLA Modules:
  0.0 105.4 jit_solution(12110716585783925698)
XLA Ops:
  0.6 99.5 %layer.1 = (bf16[384,1024]{1,0:T(8,128)(2,1)}, bf16[384,1024]{1,0:T(8,128)(2,1)}, f32[1,10240]{1,0:T(1,128)}) custom-call(bf16[384,1024]{1,0:T(8,128)(2,1)} %x_hbm.1, bf16[384,1024]{1,0:T(8,128)(2,1)} %og_hbm.1, f32[1,1024]{1,0:T(1,128)} %bitcast.15, f32[1,1024]{1,0:T(1,128)} %bitcast.16, f32[64,160]{1,0:T(8,128)} %bitcast.11, s32[1536]{0:T(1024)} %seg_hbm.1, ...), custom_call_target="tpu_custom_call" | custom-call | tf_op jit(solution)/shard_map/layer/pallas_call | solution.py:1069
  100.2 5.1 %update.1 = (f32[64,160]{1,0:T(8,128)}, f32[1,1]{1,0:T(1,128)}, f32[64,160]{1,0:T(8,128)}, bf16[64,160]{1,0:T(8,128)(2,1)}, f32[64,160]{1,0:T(8,128)}, /*index=5...) custom-call(f32[1,10240]{1,0:T(1,128)} %get-tuple-element.19.raw, f32[64,160]{1,0:T(8,128)} %bitcast.12, ...), custom_call_target="tpu_custom_call" | custom-call | tf_op jit(solution)/shard_map/update/pallas_call | solution.py:1187

commit v6 on v5

--- a/solution.py
+++ b/solution.py
@@ -714,7 +714,7 @@
             hid[r, :, pl.ds(n, TILE)] = grad.astype(BF16)
         return carry
 
-    lax.fori_loop(0, T, ffn_back, 0)
+    lax.fori_loop(0, T, ffn_back, 0, unroll=2)
     for n in range(0, D, TILE):
         total = nt(hid[0], w1(0)[n : n + TILE, :])
         for r in range(1, T):
@@ -902,7 +902,7 @@
     lax.fori_loop(0, T, rank_back_pair, 0)
     part_first = jnp.where(lone == 0, 1, 0)
 
-    lax.fori_loop(0, T, rank_back_lone, 0)
+    lax.fori_loop(0, T, rank_back_lone, 0, unroll=2)
     late.start()
 
     def halves(k, carry):

time: 106 us -> 106 us (level)
  no operation moved by 1% of the time
where the time goes in v6:
time: 106 us; the launch traced here: 105 us
  Pallas kernels  104 us (98%)
    pallas_call x1, Pallas kernels, layer_call(): pl.pallas_call(partial(layer_kernel, lay), out_shape=(jax.ShapeDtypeStruc...  98.7 us
    pallas_call x1, Pallas kernels, update_call(): pl.pallas_call(update_kernel, out_shape=(block, jax.ShapeDtypeStruct((1,...  5.06 us

profile of v6, /device:TPU:0, one launch (start us, length us, event | category | flops | bytes accessed | tf_op | source)
XLA Modules:
  0.0 104.5 jit_solution(4926847158014182677)
XLA Ops:
  0.6 98.7 %layer.1 = (bf16[384,1024]{1,0:T(8,128)(2,1)}, bf16[384,1024]{1,0:T(8,128)(2,1)}, f32[1,10240]{1,0:T(1,128)}) custom-call(bf16[384,1024]{1,0:T(8,128)(2,1)} %x_hbm.1, bf16[384,1024]{1,0:T(8,128)(2,1)} %og_hbm.1, f32[1,1024]{1,0:T(1,128)} %bitcast.15, f32[1,1024]{1,0:T(1,128)} %bitcast.16, f32[64,160]{1,0:T(8,128)} %bitcast.11, s32[1536]{0:T(1024)} %seg_hbm.1, ...), custom_call_target="tpu_custom_call" | custom-call | tf_op jit(solution)/shard_map/layer/pallas_call | solution.py:1069
  99.3 5.1 %update.1 = (f32[64,160]{1,0:T(8,128)}, f32[1,1]{1,0:T(1,128)}, f32[64,160]{1,0:T(8,128)}, bf16[64,160]{1,0:T(8,128)(2,1)}, f32[64,160]{1,0:T(8,128)}, /*index=5...) custom-call(f32[1,10240]{1,0:T(1,128)} %get-tuple-element.19.raw, f32[64,160]{1,0:T(8,128)} %bitcast.12, ...), custom_call_target="tpu_custom_call" | custom-call | tf_op jit(solution)/shard_map/update/pallas_call | solution.py:1187

commit v7 on v6

--- a/solution.py
+++ b/solution.py
@@ -714,7 +714,7 @@
             hid[r, :, pl.ds(n, TILE)] = grad.astype(BF16)
         return carry
 
-    lax.fori_loop(0, T, ffn_back, 0, unroll=2)
+    lax.fori_loop(0, T, ffn_back, 0, unroll=4 if quads else 2)
     for n in range(0, D, TILE):
         total = nt(hid[0], w1(0)[n : n + TILE, :])
         for r in range(1, T):
@@ -902,7 +902,7 @@
     lax.fori_loop(0, T, rank_back_pair, 0)
     part_first = jnp.where(lone == 0, 1, 0)
 
-    lax.fori_loop(0, T, rank_back_lone, 0, unroll=2)
+    lax.fori_loop(0, T, rank_back_lone, 0, unroll=4 if quads else 2)
     late.start()
 
     def halves(k, carry):
@@ -1085,7 +1085,7 @@
 
 VMEM_BYTES = 63 * 2**20
 PLAN = [2, 5, 3, 6]
-PARTS = 4
+PARTS = 1
 
 
 def update_kernel(

time: 106 us -> 105 us (level)
  no operation moved by 1% of the time
where the time goes in v7:
time: 105 us; the launch traced here: 104 us
  Pallas kernels  103 us (98%)
    pallas_call x1, Pallas kernels, layer_call(): pl.pallas_call(partial(layer_kernel, lay), out_shape=(jax.ShapeDtypeStruc...  98.2 us
    pallas_call x1, Pallas kernels, update_call(): pl.pallas_call(update_kernel, out_shape=(block, jax.ShapeDtypeStruct((1,...  4.84 us

profile of v7, /device:TPU:0, one launch (start us, length us, event | category | flops | bytes accessed | tf_op | source)
XLA Modules:
  0.0 103.9 jit_solution(6614577412782234317)
XLA Ops:
  0.6 98.2 %layer.1 = (bf16[384,1024]{1,0:T(8,128)(2,1)}, bf16[384,1024]{1,0:T(8,128)(2,1)}, f32[1,10240]{1,0:T(1,128)}) custom-call(bf16[384,1024]{1,0:T(8,128)(2,1)} %x_hbm.1, bf16[384,1024]{1,0:T(8,128)(2,1)} %og_hbm.1, f32[1,1024]{1,0:T(1,128)} %bitcast.15, f32[1,1024]{1,0:T(1,128)} %bitcast.16, f32[64,160]{1,0:T(8,128)} %bitcast.11, s32[1536]{0:T(1024)} %seg_hbm.1, ...), custom_call_target="tpu_custom_call" | custom-call | tf_op jit(solution)/shard_map/layer/pallas_call | solution.py:1069
  98.9 4.8 %update.1 = (f32[64,160]{1,0:T(8,128)}, f32[1,1]{1,0:T(1,128)}, f32[64,160]{1,0:T(8,128)}, bf16[64,160]{1,0:T(8,128)(2,1)}, f32[64,160]{1,0:T(8,128)}, /*index=5...) custom-call(f32[1,10240]{1,0:T(1,128)} %get-tuple-element.19.raw, f32[64,160]{1,0:T(8,128)} %bitcast.12, ...), custom_call_target="tpu_custom_call" | custom-call | tf_op jit(solution)/shard_map/update/pallas_call | solution.py:1187

commit v8 on v6

--- a/solution.py
+++ b/solution.py
@@ -714,7 +714,7 @@
             hid[r, :, pl.ds(n, TILE)] = grad.astype(BF16)
         return carry
 
-    lax.fori_loop(0, T, ffn_back, 0, unroll=2)
+    lax.fori_loop(0, T, ffn_back, 0, unroll=4)
     for n in range(0, D, TILE):
         total = nt(hid[0], w1(0)[n : n + TILE, :])
         for r in range(1, T):

time: 106 us -> 105 us (level)
  no operation moved by 1% of the time
where the time goes in v8:
time: 105 us; the launch traced here: 104 us
  Pallas kernels  103 us (98%)
    pallas_call x1, Pallas kernels, layer_call(): pl.pallas_call(partial(layer_kernel, lay), out_shape=(jax.ShapeDtypeStruc...  98.2 us
    pallas_call x1, Pallas kernels, update_call(): pl.pallas_call(update_kernel, out_shape=(block, jax.ShapeDtypeStruct((1,...  5.07 us

profile of v8, /device:TPU:0, one launch (start us, length us, event | category | flops | bytes accessed | tf_op | source)
XLA Modules:
  0.0 104.1 jit_solution(13677295405023943909)
XLA Ops:
  0.6 98.2 %layer.1 = (bf16[384,1024]{1,0:T(8,128)(2,1)}, bf16[384,1024]{1,0:T(8,128)(2,1)}, f32[1,10240]{1,0:T(1,128)}) custom-call(bf16[384,1024]{1,0:T(8,128)(2,1)} %x_hbm.1, bf16[384,1024]{1,0:T(8,128)(2,1)} %og_hbm.1, f32[1,1024]{1,0:T(1,128)} %bitcast.15, f32[1,1024]{1,0:T(1,128)} %bitcast.16, f32[64,160]{1,0:T(8,128)} %bitcast.11, s32[1536]{0:T(1024)} %seg_hbm.1, ...), custom_call_target="tpu_custom_call" | custom-call | tf_op jit(solution)/shard_map/layer/pallas_call | solution.py:1069
  98.8 5.1 %update.1 = (f32[64,160]{1,0:T(8,128)}, f32[1,1]{1,0:T(1,128)}, f32[64,160]{1,0:T(8,128)}, bf16[64,160]{1,0:T(8,128)(2,1)}, f32[64,160]{1,0:T(8,128)}, /*index=5...) custom-call(f32[1,10240]{1,0:T(1,128)} %get-tuple-element.19.raw, f32[64,160]{1,0:T(8,128)} %bitcast.12, ...), custom_call_target="tpu_custom_call" | custom-call | tf_op jit(solution)/shard_map/update/pallas_call | solution.py:1187
